TPU v7x, 512 devices: a whole 4x4x16 slice. The times are simulated.
512 devices in a mesh: gx: 4 (over z_lo), gy: 16 (over x, z_hi), gz: 8 (over y, core).
Axes of the slice: x: 4, y: 4, z: 16 (z_hi: 4, z_lo: 4; z = z_hi * 4 + z_lo), core: 2. Of those that a mesh axis runs over, the one named last changes fastest.
Arguments:
- e_field: float32 [3, 32, 128, 2048], P(None, 'gz', 'gx', 'gy'), may hold values from -6 to 6
- h_field: float32 [3, 32, 128, 2048], P(None, 'gz', 'gx', 'gy'), may hold values from -6 to 6
- pole_current: float32 [3, 32, 128, 2048], P(None, 'gz', 'gx', 'gy'), may hold values from -6 to 6
- material: int32 [32, 128, 2048], P('gz', 'gx', 'gy'), may hold values from 0 to 3
- pole_table: float32 [3, 4], replicated, may hold values from 0.2 to 0.9
- cotangent: float32 [16, 8, 4096], P(None, None, ('gx', 'gy', 'gz')), may hold values from -6 to 6
- cosines: float32 [2, 4096], P(None, ('gx', 'gy', 'gz')), may hold values from -0.7 to 0.7
- wavenumber: float32 [16], replicated, may hold values from 0.6 to 0.8
- time_phase: float32 [16], replicated, may hold values from -3.140625 to 3.140625
Outputs:
- e_next: float32 [3, 32, 128, 2048], P(None, 'gz', 'gx', 'gy')
- h_next: float32 [3, 32, 128, 2048], P(None, 'gz', 'gx', 'gy')
- pole_next: float32 [3, 32, 128, 2048], P(None, 'gz', 'gx', 'gy')
All inputs are finite; a program needn't handle non-finite values.
Results may differ from a plain program's by a relative error of at most 0.0003.
Values sent between devices are 32-bit elements; how exact they have to be, the bound alone decides.
A program may use at most 64 MiB of HBM per device.

v0:
```python
import math

import jax
import jax.numpy as jnp
from jax import lax
from jax.sharding import PartitionSpec as P

FREQS = 16
DIRS = 4096
NPOLE = 4


courant = 0.5


def turned_gather(arrays, axis, dims):
    turned = [jnp.moveaxis(a, dim, 0) for a, dim in zip(arrays, dims)]
    widths = [t[0].size for t in turned]
    both = jnp.concatenate([t.reshape(-1, w) for t, w in zip(turned, widths)], axis=1)
    filled = lax.all_gather(both, axis, axis=0, tiled=True)
    tiles = jnp.split(filled, [sum(widths[:k]) for k in range(1, len(widths))], axis=1)
    return tuple(
        (
            jnp.moveaxis(b.reshape(-1, *t.shape[1:]), 0, dim)
            for b, t, dim in zip(tiles, turned, dims)
        )
    )


def copy_for_each(array, axis):
    copies = jnp.broadcast_to(array, (lax.axis_size(axis), *array.shape))
    return lax.all_to_all(copies, axis, split_axis=0, concat_axis=0, tiled=True)


def of_everyone(array, axis):
    return copy_for_each(array, axis).sum(axis=0)


def from_behind(array, axis, by):
    size = lax.axis_size(axis)
    pairs = [(i, i + by) for i in range(size) if 0 <= i + by < size]
    return lax.ppermute(array, axis, pairs)


def surface_source(cotangent, cosines, wavenumber, time_phase, xs, ys):
    count = cotangent.shape[2]
    rows_x = xs.shape[0]
    rows_y = ys.shape[0]

    def one_freq(total, freq):
        wave = wavenumber[freq]
        along_x = wave * cosines[0]
        along_y = wave * cosines[1]
        phase_x = xs[:, None] * along_x[None, :] - time_phase[freq]
        phase_y = ys[:, None] * along_y[None, :]
        cos_x = jnp.cos(phase_x)[None]
        sin_x = jnp.sin(phase_x)[None]
        weights = cotangent[freq]
        real_part = weights[0::2][:, None, :]
        imag_part = weights[1::2][:, None, :]
        first = real_part * cos_x - imag_part * sin_x
        second = -(real_part * sin_x + imag_part * cos_x)
        left = jnp.concatenate([first, second], axis=2).reshape(4 * rows_x, 2 * count)
        right = jnp.concatenate([jnp.cos(phase_y), jnp.sin(phase_y)], axis=1).T
        part = jnp.dot(
            left, right, preferred_element_type=jnp.float32, precision=lax.Precision.HIGHEST
        )
        return (total + part.reshape(4, rows_x, rows_y), None)

    start = jnp.zeros((4, rows_x, rows_y), jnp.float32)
    total, _ = lax.scan(one_freq, start, jnp.arange(cotangent.shape[0], dtype=jnp.int32))
    return total


def ahead(value, nearby, axis):
    rest = lax.slice_in_dim(value, 1, value.shape[axis], axis=axis)
    return jnp.concatenate([rest, nearby], axis) - value


def behind(value, nearby, axis):
    rest = lax.slice_in_dim(value, 0, value.shape[axis] - 1, axis=axis)
    return value - jnp.concatenate([nearby, rest], axis)


def local(
    e_field, h_field, pole_current, material, pole_table, cotangent, cosines, wavenumber, time_phase
):
    depth, width_x, width_y = material.shape
    scale = 1.0 / math.sqrt(DIRS * FREQS)
    anchor_x = (lax.axis_index("gx") * width_x).astype(jnp.float32)
    anchor_y = (lax.axis_index("gy") * width_y).astype(jnp.float32)
    ys = anchor_y + jnp.arange(width_y).astype(jnp.float32)
    first_cot, first_cos = turned_gather((cotangent, cosines), "gx", (2, 1))
    band_cot, band_cos = turned_gather((first_cot, first_cos), "gy", (2, 1))
    xs = anchor_x + jnp.arange(width_x).astype(jnp.float32)
    partial_value = surface_source(band_cot, band_cos, wavenumber, time_phase, xs, ys)
    source = of_everyone(partial_value, "gz") * scale
    is_top = lax.axis_index("gz") == lax.axis_size("gz") - 1
    top = ((jnp.arange(depth) == depth - 1) & is_top).astype(jnp.float32)[:, None, None]
    next_x = from_behind(e_field[1:3, :, :1, :], "gx", -1)
    next_y = from_behind(e_field[0::2, :, :, :1], "gy", -1)
    next_z = from_behind(e_field[0:2, :1], "gz", -1)
    ex, ey, ez = (e_field[0], e_field[1], e_field[2])
    curl_x = ahead(ez, next_y[1], 2) - ahead(ey, next_z[1], 0)
    curl_y = ahead(ex, next_z[0], 0) - ahead(ez, next_x[1], 1)
    curl_z = ahead(ey, next_x[0], 1) - ahead(ex, next_y[0], 2)
    hx = h_field[0] - courant * curl_x - courant * top * source[2][None]
    hy = h_field[1] - courant * curl_y - courant * top * source[3][None]
    hz = h_field[2] - courant * curl_z
    h_next = jnp.stack([hx, hy, hz])
    prev_x = from_behind(h_next[1:3, :, -1:, :], "gx", 1)
    prev_y = from_behind(h_next[0::2, :, :, -1:], "gy", 1)
    prev_z = from_behind(h_next[0:2, -1:], "gz", 1)
    chosen = (material[None] == jnp.arange(NPOLE, dtype=jnp.int32)[:, None, None, None]).astype(
        jnp.float32
    )
    decay = jnp.sum(chosen * pole_table[0][:, None, None, None], axis=0)
    drive = jnp.sum(chosen * pole_table[1][:, None, None, None], axis=0)
    coef = jnp.sum(chosen * pole_table[2][:, None, None, None], axis=0)
    pole_next = decay[None] * pole_current + drive[None] * e_field
    side_x = behind(hz, prev_y[1], 2) - behind(hy, prev_z[1], 0)
    side_y = behind(hx, prev_z[0], 0) - behind(hz, prev_x[1], 1)
    side_z = behind(hy, prev_x[0], 1) - behind(hx, prev_y[0], 2)
    curl_h = jnp.stack([side_x, side_y, side_z])
    inject = jnp.stack([top * source[0][None], top * source[1][None], jnp.zeros_like(ex)])
    e_next = (
        e_field + coef[None] * (curl_h - 0.5 * (pole_next + pole_current)) - coef[None] * inject
    )
    return (e_next, h_next, pole_next)


def solution(mesh):
    in_specs = (
        P(None, "gz", "gx", "gy"),
        P(None, "gz", "gx", "gy"),
        P(None, "gz", "gx", "gy"),
        P("gz", "gx", "gy"),
        P(),
        P(None, None, ("gx", "gy", "gz")),
        P(None, ("gx", "gy", "gz")),
        P(),
        P(),
    )
    out_specs = (P(None, "gz", "gx", "gy"), P(None, "gz", "gx", "gy"), P(None, "gz", "gx", "gy"))
    return jax.shard_map(local, mesh=mesh, in_specs=in_specs, out_specs=out_specs, check_vma=False)
```

profile of v0, /device:TPU:11, one launch (start us, length us, event | category | flops | bytes accessed | tf_op | source)
XLA Modules:
  0.0 227.1 jit_solution(3024068051090232866)
XLA Ops:
  0.6 0.8 copy.38
  2.2 11.3 %all_gather.6 = f32[32,130]{1,0:T(8,128)S(1)} all-gather(f32[8,130]{1,0:T(8,128)S(1)} %pad_maximum_fusion.2), channel_id=1, replica_groups=mesh['gx'=4,'gy'=16,'gz'=8] {'gx'}, dimensions={0}, use_global_device_ids=true | all-gather | bytes 20800 | tf_op jit(solution)/shard_map/all_gather | solution.py:20
  13.6 52.0 %all_gather.7 = f32[512,130]{1,0:T(8,128)S(1)} all-gather(f32[32,130]{1,0:T(8,128)S(1)} %all_gather.6), channel_id=1, replica_groups=mesh['gx'=4,'gy'=16,'gz'=8] {'gy'}, dimensions={0}, use_global_device_ids=true | all-gather | bytes 282880 | tf_op jit(solution)/shard_map/all_gather | solution.py:20
  66.6 106.9 %while.11 = (s32[]{:T(128)}, f32[4,32,128]{2,1,0:T(8,128)S(1)}, s32[16]{0:T(128)S(1)}, f32[16,8,512]{2,1,0:T(8,128)S(1)}, f32[16]{0:T(128)S(1)}, /*index=5*/f32[...) while((s32[]{:T(128)}, f32[4,32,128]{2,1,0:T(8,128)S(1)}, ...), condition=%wide.region_2.3_spmd.clone, body=%wide.region_1.2_spmd.clone.sunk | while | flops 202179904 | bytes 2586073 | solution.py:71
  70.6 0.9 fusion.51
  71.6 1.0 multiply_cosine_fusion.2
  77.3 0.9 fusion.51
  78.3 1.0 multiply_cosine_fusion.2
  84.0 0.9 fusion.51
  85.0 1.0 multiply_cosine_fusion.2
  90.7 0.9 fusion.51
  91.7 1.0 multiply_cosine_fusion.2
  97.3 0.9 fusion.51
  98.4 1.0 multiply_cosine_fusion.2
  104.0 0.9 fusion.51
  105.0 1.0 multiply_cosine_fusion.2
  110.7 0.9 fusion.51
  111.7 1.0 multiply_cosine_fusion.2
  117.4 0.9 fusion.51
  118.4 1.0 multiply_cosine_fusion.2
  124.1 0.9 fusion.51
  125.1 1.0 multiply_cosine_fusion.2
  130.7 0.9 fusion.51
  131.8 1.0 multiply_cosine_fusion.2
  137.4 0.9 fusion.51
  138.5 1.0 multiply_cosine_fusion.2
  144.1 0.9 fusion.51
  145.1 1.0 multiply_cosine_fusion.2
  150.8 0.9 fusion.51
  151.8 1.0 multiply_cosine_fusion.2
  157.5 0.9 fusion.51
  158.5 1.0 multiply_cosine_fusion.2
  164.2 0.9 fusion.51
  165.2 1.0 multiply_cosine_fusion.2
  170.8 0.9 fusion.51
  171.9 1.0 multiply_cosine_fusion.2
  173.5 0.9 broadcast_in_dim.5
  174.3 15.4 %all-to-all-start = ((f32[8,4,32,128]{3,2,1,0:T(8,128)}), f32[8,4,32,128]{3,2,1,0:T(8,128)S(1)}, u32[]{:S(2)}, u32[]{:S(2)}) async-start(f32[8,4,32,128]{3,2,1,0:T(8,128)} %broadcast_in_dim.5), calls=%async_computation | async-start | bytes 1048576 | tf_op jit(solution)/shard_map/all_to_all | solution.py:32
  189.8 5.1 %collective-permute-start.1 = (f32[2,4,32,1]{3,2,1,0:T(8,128)S(1)}, f32[2,4,32,1]{3,2,1,0:T(8,128)S(1)}, u32[]{:S(2)}, u32[]{:S(2)}) collective-permute-start(f32[2,4,32,1]{3,2,1,0:T(8,128)S(1)} %slice.160), channel_id=1, source_target_pairs={{8,0},{16,8},{24,16},{32,24},{40,32},{48,40},{56,48},{64,56},{72,6... | collective-permute-start | bytes 3080 | tf_op jit(solution)/shard_map/ppermute | solution.py:42
  194.9 2.5 %collective-permute-start.2 = (f32[2,1,32,128]{3,2,1,0:T(8,128)S(1)}, f32[2,1,32,128]{3,2,1,0:T(8,128)S(1)}, u32[]{:S(2)}, u32[]{:S(2)}) collective-permute-start(f32[2,1,32,128]{3,2,1,0:T(8,128)S(1)} %slice.167), channel_id=1, source_target_pairs={{1,0},{2,1},{3,2},{4,3},{5,4},{6,5},{7,6},{9,8},{10,9},{11,10},{12... | collective-permute-start | bytes 98312 | tf_op jit(solution)/shard_map/ppermute | solution.py:42
  197.5 1.3 collective-permute-start
  200.0 6.9 %collective-permute-done.1 = f32[2,4,32,1]{3,2,1,0:T(8,128)S(1)} collective-permute-done((f32[2,4,32,1]{3,2,1,0:T(8,128)S(1)}, f32[2,4,32,1]{3,2,1,0:T(8,128)S(1)}, u32[]{:S(2)}, u32[]{:S(2)}) %collective-permute-start.1) | collective-permute-done | bytes 1056 | tf_op jit(solution)/shard_map/ppermute | solution.py:42
  207.1 0.9 copy-done.1
  209.1 2.3 %collective-permute-start.3 = (f32[2,4,32,1]{3,2,1,0:T(8,128)S(1)}, f32[2,4,32,1]{3,2,1,0:T(8,128)S(1)}, u32[]{:S(2)}, u32[]{:S(2)}) collective-permute-start(f32[2,4,32,1]{3,2,1,0:T(8,128)S(1)} %slice.176), channel_id=1, source_target_pairs={{0,8},{8,16},{16,24},{24,32},{32,40},{40,48},{48,56},{56,64},{64,7... | collective-permute-start | bytes 3080 | tf_op jit(solution)/shard_map/ppermute | solution.py:42
  211.4 1.3 collective-permute-start.5
  212.7 5.2 %collective-permute-start.4 = (f32[2,1,32,128]{3,2,1,0:T(8,128)S(1)}, f32[2,1,32,128]{3,2,1,0:T(8,128)S(1)}, u32[]{:S(2)}, u32[]{:S(2)}) collective-permute-start(f32[2,1,32,128]{3,2,1,0:T(8,128)S(1)} %pad_maximum_fusion.1), channel_id=1, source_target_pairs={{0,1},{1,2},{2,3},{3,4},{4,5},{5,6},{6,7},{8,9},{9,10},{10,11},{11... | collective-permute-start | bytes 98312 | tf_op jit(solution)/shard_map/ppermute | solution.py:42
  218.0 7.3 %collective-permute-done.3 = f32[2,4,32,1]{3,2,1,0:T(8,128)S(1)} collective-permute-done((f32[2,4,32,1]{3,2,1,0:T(8,128)S(1)}, f32[2,4,32,1]{3,2,1,0:T(8,128)S(1)}, u32[]{:S(2)}, u32[]{:S(2)}) %collective-permute-start.3) | collective-permute-done | bytes 1056 | tf_op jit(solution)/shard_map/ppermute | solution.py:42
  226.2 0.8 fusion.14
  (243 shorter events, 53.7 us)
Async XLA Ops:
  1.5 0.7 copy-start.6
  65.9 0.7 copy-start.7
  65.9 0.7 copy-start.8
  174.3 15.4 %copy-start = (f32[3,4,32,128]{3,2,1,0:T(8,128)S(1)}, f32[3,4,32,128]{3,2,1,0:T(8,128)}, u32[]{:S(2)}) copy-start(f32[3,4,32,128]{3,2,1,0:T(8,128)} %param.11) | copy-start | bytes 589828
  174.3 32.6 %all-to-all-start = ((f32[8,4,32,128]{3,2,1,0:T(8,128)}), f32[8,4,32,128]{3,2,1,0:T(8,128)S(1)}, u32[]{:S(2)}, u32[]{:S(2)}) async-start(f32[8,4,32,128]{3,2,1,0:T(8,128)} %broadcast_in_dim.5), calls=%async_computation | async-start | bytes 1048576 | tf_op jit(solution)/shard_map/all_to_all | solution.py:32
  189.8 17.1 %collective-permute-start.1 = (f32[2,4,32,1]{3,2,1,0:T(8,128)S(1)}, f32[2,4,32,1]{3,2,1,0:T(8,128)S(1)}, u32[]{:S(2)}, u32[]{:S(2)}) collective-permute-start(f32[2,4,32,1]{3,2,1,0:T(8,128)S(1)} %slice.160), channel_id=1, source_target_pairs={{8,0},{16,8},{24,16},{32,24},{40,32},{48,40},{56,48},{64,56},{72,6... | collective-permute-start | bytes 3080 | tf_op jit(solution)/shard_map/ppermute | solution.py:42
  194.9 12.0 %collective-permute-start.2 = (f32[2,1,32,128]{3,2,1,0:T(8,128)S(1)}, f32[2,1,32,128]{3,2,1,0:T(8,128)S(1)}, u32[]{:S(2)}, u32[]{:S(2)}) collective-permute-start(f32[2,1,32,128]{3,2,1,0:T(8,128)S(1)} %slice.167), channel_id=1, source_target_pairs={{1,0},{2,1},{3,2},{4,3},{5,4},{6,5},{7,6},{9,8},{10,9},{11,10},{12... | collective-permute-start | bytes 98312 | tf_op jit(solution)/shard_map/ppermute | solution.py:42
  197.5 9.5 %collective-permute-start = (f32[2,4,1,128]{3,2,1,0:T(1,128)S(1)}, f32[2,4,1,128]{3,2,1,0:T(1,128)S(1)}, u32[]{:S(2)}, u32[]{:S(2)}) collective-permute-start(f32[2,4,1,128]{3,2,1,0:T(1,128)S(1)} %slice.156), channel_id=1, source_target_pairs={{128,0},{256,128},{384,256},{129,1},{257,129},{385,257},{130,2},{2... | collective-permute-start | bytes 12296 | tf_op jit(solution)/shard_map/ppermute | solution.py:42
  198.9 0.8 copy-start.4
  198.9 0.7 copy-start.5
  207.0 0.9 copy-start.1
  208.3 0.7 copy-start.2
  209.1 16.2 %collective-permute-start.3 = (f32[2,4,32,1]{3,2,1,0:T(8,128)S(1)}, f32[2,4,32,1]{3,2,1,0:T(8,128)S(1)}, u32[]{:S(2)}, u32[]{:S(2)}) collective-permute-start(f32[2,4,32,1]{3,2,1,0:T(8,128)S(1)} %slice.176), channel_id=1, source_target_pairs={{0,8},{8,16},{16,24},{24,32},{32,40},{40,48},{48,56},{56,64},{64,7... | collective-permute-start | bytes 3080 | tf_op jit(solution)/shard_map/ppermute | solution.py:42
  211.4 13.9 %collective-permute-start.5 = (f32[2,4,1,128]{3,2,1,0:T(1,128)S(1)}, f32[2,4,1,128]{3,2,1,0:T(1,128)S(1)}, u32[]{:S(2)}, u32[]{:S(2)}) collective-permute-start(f32[2,4,1,128]{3,2,1,0:T(1,128)S(1)} %pad_maximum_fusion.3), channel_id=1, source_target_pairs={{0,128},{128,256},{256,384},{1,129},{129,257},{257,385},{2,130},{1... | collective-permute-start | bytes 12296 | tf_op jit(solution)/shard_map/ppermute | solution.py:42
  212.7 12.6 %collective-permute-start.4 = (f32[2,1,32,128]{3,2,1,0:T(8,128)S(1)}, f32[2,1,32,128]{3,2,1,0:T(8,128)S(1)}, u32[]{:S(2)}, u32[]{:S(2)}) collective-permute-start(f32[2,1,32,128]{3,2,1,0:T(8,128)S(1)} %pad_maximum_fusion.1), channel_id=1, source_target_pairs={{0,1},{1,2},{2,3},{3,4},{4,5},{5,6},{6,7},{8,9},{9,10},{10,11},{11... | collective-permute-start | bytes 98312 | tf_op jit(solution)/shard_map/ppermute | solution.py:42
  225.3 0.9 copy-start.3
where the time goes:
time: 228 us; the launch traced here: 227 us
  blocking collectives  63.3 us (28%)
  other arithmetic  41.8 us (18%)
  local copies, waits for them, and re-layouts  35.4 us (16%)
  starting transfers between devices  33.1 us (15%)
  loops' own time  28.5 us (12%)
  waiting for transfers between devices  14.2 us (6%)
  matrix products  9.66 us (4%)
    all_gather x2, blocking collectives, turned_gather(): filled = lax.all_gather(both, axis, axis=0, tiled=True)  63.3 us
    another operation x1, loops' own time, surface_source(): lax.scan(one_freq, start, jnp.arange(cotangent.shape[0], dtype=jnp.int32))  28.5 us
    ppermute x6, starting transfers between devices, from_behind(): return lax.ppermute(array, axis, pairs)  17.7 us
    cos x16, other arithmetic, one_freq(): right = jnp.concatenate([jnp.cos(phase_y), jnp.sin(phase_y)], axis=1).T  15.7 us
    all_to_all x1, starting transfers between devices, copy_for_each(): return lax.all_to_all(copies, axis, split_axis=0, concat_axis=0, tiled=True)  15.4 us
    ppermute x6, waiting for transfers between devices, from_behind(): return lax.ppermute(array, axis, pairs)  14.2 us
    cos x16, other arithmetic, one_freq(): cos_x = jnp.cos(phase_x)[None]  14 us
    dot_general x16, matrix products, one_freq(): jnp.dot(left, right, preferred_element_type=jnp.float32, precision=lax.Pr...  9.66 us
  transfers between devices with their start and end apart: 7, of which 2 were waited for; matrix products, arithmetic and copies ran while one was open for 0% of the time, Pallas kernels for 0%

commit v1 on v0

v1 whole, which is shorter than its diff:
```python
import functools
import math

import jax
import jax.numpy as jnp
from jax import lax
from jax.experimental import pallas as pl
from jax.experimental.pallas import tpu as pltpu
from jax.sharding import PartitionSpec as P

PLANES = 4
COURANT = 0.5
MESH = pl.DeviceIdType.MESH
F32 = jnp.float32
BF16 = jnp.bfloat16

TURN = 2.0 * math.pi
TURN_HI = 6.28125
TURN_LO = TURN - TURN_HI


def sincos(phase):
    turns = jnp.floor(phase * (1.0 / TURN) + 0.5)
    rest = ((phase - turns * TURN_HI) - turns * TURN_LO) * 0.25
    sq = rest * rest
    sin = rest + rest * sq * (
        -1.6666654611e-1 + sq * (8.3321608736e-3 + sq * -1.9515295891e-4)
    )
    cos = 1.0 - 0.5 * sq + sq * sq * (
        4.166664568298827e-2 + sq * (-1.388731625493765e-3 + sq * 2.443315711809948e-5)
    )
    for _ in range(2):
        sin, cos = 2.0 * sin * cos, 1.0 - 2.0 * sin * sin
    return sin, cos


def times(a, b):
    return a[0] * b[0] - a[1] * b[1], a[0] * b[1] + a[1] * b[0]


def split(value):
    high = value.astype(BF16)
    return high, (value - high.astype(F32)).astype(BF16)


def iota(shape, dim):
    return lax.broadcasted_iota(jnp.int32, shape, dim)


def kernel(
    sizes, cot_in, cosines_in, wave_in, phase_in, table_in, e_in, h_in, p_in, m_in,
    e_out, h_out, p_out, cot, cosines, wave, phase, table, e_buf, h_buf, p_buf, m_buf, gat, xs, pq, yt, lt, part, total, from_x, from_gz, chunk, top_in,
    bound_x, bound_y, low, hx_out, hx_in, hy_out, hy_in, hz_in, kx_out, kx_in, ky_out, ky_in, kz_in,
    load_sem, gat_send, gat_recv, x_send, x_recv, gz_send, gz_recv, top_send, top_recv,
    bx_send, bx_recv, by_send, by_recv, halo_send, halo_recv,
):
    n_lo, n_hi, n_x, n_gz = sizes
    n_z = n_lo * n_hi
    depth, width_x, width_y = m_buf.shape
    half = width_x // 2
    gx, gy, gz = lax.axis_index("gx"), lax.axis_index("gy"), lax.axis_index("gz")
    z_hi = lax.rem(gy, n_hi)
    x = lax.div(gy, n_hi)
    core = lax.rem(gz, 2)
    z = z_hi * n_lo + gx
    is_top = gz == n_gz - 1

    def at(dx=0, dz=None, hi=None):
        if hi is not None:
            return {"gy": x * n_hi + lax.rem(z_hi + hi, n_hi)}
        if dz is not None:
            other = lax.rem(z + dz, n_z)
            return {"gx": lax.rem(other, n_lo), "gy": x * n_hi + lax.div(other, n_lo)}
        return {"gy": lax.rem(x + dx, n_x) * n_hi + z_hi}

    def step(axis, by):
        size = lax.axis_size(axis)
        return lax.rem(lax.axis_index(axis) + by + size, size)

    loads = [
        pltpu.make_async_copy(a, b, load_sem.at[i])
        for i, (a, b) in enumerate(
            (
                (cot_in, cot),
                (cosines_in, cosines),
                (wave_in, wave),
                (phase_in, phase),
                (e_in, e_buf),
                (h_in, h_buf),
                (p_in, p_buf),
                (m_in, m_buf),
                (table_in, table),
            )
        )
    ]
    for load in loads:
        load.start()

    if n_lo == 4:
        ring = [1, 2 + (n_z - 4) * core, n_z - 1]
    else:
        ring = [1]
    rows = n_gz and (2 * 4 * half) // n_gz

    def owner(kind, comp):
        return ((kind * 4 + comp) * half) // rows

    barrier = pltpu.get_barrier_semaphore()

    def greet(device):
        pl.semaphore_signal(barrier, inc=1, device_id=device, device_id_type=MESH)

    for k in range(1, n_hi):
        greet(at(hi=n_hi - k))
    for off in ring:
        greet(at(dz=n_z - off))
    for k in range(1, n_x):
        greet(at(dx=n_x - k))
    for k in range(1, n_gz):
        greet({"gz": step("gz", k)})
    for axis in ("gx", "gy"):
        for by in (1, -1):
            greet({axis: step(axis, by)})

    @pl.when(is_top)
    def _():
        for kind in range(2):
            greet({"gx": step("gx", -1), "gz": owner(kind, 3)})
            greet({"gy": step("gy", -1), "gz": owner(kind, 2)})

    extra = sum((gz == owner(kind, c)).astype(jnp.int32) for kind in range(2) for c in (2, 3))
    greeted = (n_hi - 1) + len(ring) + (n_x - 1) + (n_gz - 1) + 4

    for load in loads[:4]:
        load.wait()
    lane8 = iota((8, 128), 1)
    lane1 = iota((1, 128), 1)
    freq = lane1 % 16
    direction = lane1 // 16
    waves = jnp.zeros((1, 128), F32)
    times_ = jnp.zeros((1, 128), F32)
    cos_x = jnp.zeros((1, 128), F32)
    cos_y = jnp.zeros((1, 128), F32)
    for f in range(16):
        waves = jnp.where(freq == f, wave[f], waves)
        times_ = jnp.where(freq == f, phase[f], times_)
    for d in range(8):
        cos_x = jnp.where(direction == d, cosines[0, d], cos_x)
        cos_y = jnp.where(direction == d, cosines[1, d], cos_y)
    weights = jnp.concatenate([cot[:, d, :] for d in range(8)], axis=1)
    scale = 1.0 / math.sqrt(16.0 * 8 * n_lo * n_hi * n_x * n_gz)
    sin_t, cos_t = sincos(-times_)
    re = [weights[2 * c : 2 * c + 1] * scale for c in range(4)]
    im = [weights[2 * c + 1 : 2 * c + 2] * scale for c in range(4)]
    mine = gat.at[gx, z_hi]
    for c in range(4):
        mine[c : c + 1, :] = re[c] * cos_t - im[c] * sin_t
        mine[4 + c : 5 + c, :] = re[c] * sin_t + im[c] * cos_t
    mine[8:9, :] = waves * cos_x
    mine[9:10, :] = waves * cos_y

    pl.semaphore_wait(barrier, greeted + extra)

    def send(src, dst, send_sem, recv_sem, device):
        copy = pltpu.make_async_remote_copy(
            src_ref=src, dst_ref=dst, send_sem=send_sem, recv_sem=recv_sem,
            device_id=device, device_id_type=MESH,
        )
        return copy

    first = []
    for k in range(1, n_hi):
        block = gat.at[gx, z_hi, 0:10]
        copy = send(block, block, gat_send.at[k - 1], gat_recv.at[k - 1], at(hi=k))
        copy.start()
        first.append(copy)

    loads[4].wait()
    for i in range(2):
        for j in range(depth):
            hx_out[i * depth + j : i * depth + j + 1, :] = e_buf[1 + i, j, 0:1, :]
    packed = jnp.zeros((8, 128), F32)
    for i in range(2):
        for j in range(depth):
            for g in range(width_x // 8):
                to = (i * depth + j) * (width_x // 8) + g
                col = e_buf[2 * i, j, 8 * g : 8 * g + 8, :]
                packed = jnp.where(lane8 == to, pltpu.roll(col, to, 1) if to else col, packed)
    hy_out[...] = packed
    halo = [
        send(hx_out, hx_in, halo_send.at[0], halo_recv.at[0], {"gx": step("gx", -1)}),
        send(hy_out, hy_in, halo_send.at[1], halo_recv.at[1], {"gy": step("gy", -1)}),
        send(e_buf.at[0:2, 0], hz_in, halo_send.at[2], halo_recv.at[2], {"gz": step("gz", -1)}),
    ]
    for copy in halo:
        copy.start()

    for copy in first:
        copy.wait_recv()
    second = []
    for k, off in enumerate(ring):
        block = gat.at[gx, :, 0:10]
        copy = send(block, block, gat_send.at[3 + k], gat_recv.at[3 + k], at(dz=off))
        copy.start()
        second.append(copy)

    loads[5].wait()
    for copy in halo:
        copy.wait_recv()
    row = iota((width_x, 128), 0)
    lane = iota((width_x, 128), 1)
    keep_x = (gx < lax.axis_size("gx") - 1).astype(F32)
    keep_y = (gy < lax.axis_size("gy") - 1).astype(F32)
    keep_z = (gz < n_gz - 1).astype(F32)
    groups = width_x // 8

    def column(packed, which, lane_to):
        cols = []
        for g in range(groups):
            at_lane = which * groups + g
            by = (lane_to - at_lane) % 128
            cols.append(pltpu.roll(packed, by, 1) if by else packed)
        return jnp.concatenate(cols, axis=0)

    y_packed = hy_in[...] * keep_y
    for j in range(depth):
        ex, ey, ez = e_buf[0, j], e_buf[1, j], e_buf[2, j]
        if j < depth - 1:
            ex_z, ey_z = e_buf[0, j + 1], e_buf[1, j + 1]
        else:
            ex_z, ey_z = hz_in[0] * keep_z, hz_in[1] * keep_z

        def up_x(v, i):
            edge = hx_in[i * depth + j : i * depth + j + 1, :] * keep_x
            return jnp.where(row == width_x - 1, edge, pltpu.roll(v, width_x - 1, 0)) - v

        def up_y(v, i):
            edge = column(y_packed, i * depth + j, 127)
            return jnp.where(lane == 127, edge, pltpu.roll(v, 127, 1)) - v

        curl_x = up_y(ez, 1) - (ey_z - ey)
        curl_y = (ex_z - ex) - up_x(ez, 1)
        curl_z = up_x(ey, 0) - up_y(ex, 0)
        h_buf[0, j] = h_buf[0, j] - COURANT * curl_x
        h_buf[1, j] = h_buf[1, j] - COURANT * curl_y
        h_buf[2, j] = h_buf[2, j] - COURANT * curl_z

    for i in range(2):
        for j in range(depth):
            kx_out[i * depth + j : i * depth + j + 1, :] = h_buf[
                1 + i, j, width_x - 1 : width_x, :
            ]
    packed = jnp.zeros((8, 128), F32)
    for i in range(2):
        for j in range(depth):
            for g in range(groups):
                to = (i * depth + j) * groups + g
                col = h_buf[2 * i, j, 8 * g : 8 * g + 8, :]
                packed = jnp.where(lane8 == to, pltpu.roll(col, to + 1, 1), packed)
    ky_out[...] = packed
    halo2 = [
        send(kx_out, kx_in, halo_send.at[3], halo_recv.at[3], {"gx": step("gx", 1)}),
        send(ky_out, ky_in, halo_send.at[4], halo_recv.at[4], {"gy": step("gy", 1)}),
        send(
            h_buf.at[0:2, depth - 1], kz_in, halo_send.at[5], halo_recv.at[5],
            {"gz": step("gz", 1)},
        ),
    ]
    for copy in halo2:
        copy.start()

    for copy in second:
        copy.wait_recv()
    row8 = iota((8, 128), 0)
    rowf = row8.astype(F32)
    centre = (gx * width_x).astype(F32) + (0.5 * width_x - 0.5)
    tile_y = ((row8 * n_hi + z_hi) * width_y).astype(F32)
    mul_x = jnp.where(row8 < 4, centre, jnp.where(row8 == 7, 8.0, 0.0))
    mul_y = jnp.where(
        row8 < 4,
        tile_y,
        jnp.where(row8 == 4, 8.0, jnp.where(row8 == 5, 32.0, jnp.where(row8 == 6, 64.0, 0.0))),
    )
    sign = jnp.where(row8 < 4, -1.0, 1.0)

    def factors(s, carry):
        lo = lax.div(s, n_hi)
        hi = lax.rem(s, n_hi)
        along_x = gat[lo, hi, 8:9, :]
        along_y = gat[lo, hi, 9:10, :]
        w = gat[lo, hi, 0:8, :]
        turned = pltpu.roll(w, 4, 0) * sign
        sin_m, cos_m = sincos(along_x * mul_x + along_y * mul_y)
        for t in range(n_x):
            pq[t, s] = w * cos_m[t : t + 1] + turned * sin_m[t : t + 1]
        sin_b, cos_b = sincos(along_x * (rowf + 0.5))
        more = times((cos_b, sin_b), (cos_m[7:8], sin_m[7:8]))
        xs[s, 0, 0:8] = cos_b
        xs[s, 0, 8:16] = more[0]
        xs[s, 1, 0:8] = sin_b
        xs[s, 1, 8:16] = more[1]
        sin_b, cos_b = sincos(along_y * rowf)
        e8 = (cos_m[4:5], sin_m[4:5])
        more = times((cos_b, sin_b), e8)
        block = (jnp.concatenate([cos_b, more[0]], 0), jnp.concatenate([sin_b, more[1]], 0))
        blocks = [block]
        for power in (times(e8, e8), (cos_m[5:6], sin_m[5:6]), (cos_m[6:7], sin_m[6:7])):
            blocks = blocks + [times(b, power) for b in blocks]
        for g, b in enumerate(blocks):
            for kind in range(2):
                high, lowp = split(b[kind])
                base = pl.multiple_of(s * 256 + kind * 128, 128)
                yt[16 * g : 16 * g + 16, pl.ds(base, 128)] = high
                yt[128 + 16 * g : 144 + 16 * g, pl.ds(base, 128)] = lowp
        return carry

    lax.fori_loop(0, n_z, factors, 0)

    def tile(t):
        def build(s, carry):
            cx, sx = xs[s, 0], xs[s, 1]
            nx = -sx
            for c in range(4):
                p = pq[t, s, c : c + 1, :]
                nq = -pq[t, s, 4 + c : 5 + c, :]
                products = ((p * cx, nq * cx), (nq * sx, p * nx))
                for kind in range(2):
                    r = (kind * 4 + c) * half
                    for k in range(2):
                        high, lowp = split(products[kind][k])
                        base = pl.multiple_of(s * 256 + k * 128, 128)
                        lt[r : r + half, pl.ds(base, 128)] = high
                        lt[128 + r : 128 + r + half, pl.ds(base, 128)] = lowp
            return carry

        lax.fori_loop(0, n_z, build, 0)
        both = lax.dot_general(
            lt[...], yt[...], (((1,), (1,)), ((), ())), preferred_element_type=F32
        )
        return both[0:128, 0:128] + (both[0:128, 128:256] + both[128:256, 0:128])

    def to_x(k):
        return send(
            part.at[k - 1], from_x.at[k - 1], x_send.at[k - 1], x_recv.at[k - 1],
            {"gy": lax.rem(x + k, n_x) * n_hi + z_hi},
        )

    def other(k, carry):
        part[k - 1] = tile(lax.rem(x + k, n_x))
        to_x(k).start()
        return carry

    lax.fori_loop(1, n_x, other, 0)
    own = tile(x)

    for k in range(1, n_x):
        to_x(k).wait_recv()
        own = own + from_x[k - 1]
    total[...] = own

    spread = []
    for k in range(1, n_gz):
        to = step("gz", k)
        copy = send(
            total.at[pl.ds(pl.multiple_of(to * rows, rows), rows)], from_gz.at[k - 1],
            gz_send.at[k - 1], gz_recv.at[k - 1], {"gz": to},
        )
        copy.start()
        spread.append(copy)

    for load in loads[6:]:
        load.wait()
    for copy in halo2:
        copy.wait_recv()
    keep_x = (gx > 0).astype(F32)
    keep_y = (gy > 0).astype(F32)
    keep_z = (gz > 0).astype(F32)
    y_packed = ky_in[...] * keep_y

    def chosen(which, m):
        value = jnp.full(m.shape, table[which, 3], F32)
        for i in range(3):
            value = jnp.where(m == i, table[which, i], value)
        return value

    for j in range(depth):
        hx, hy, hz = h_buf[0, j], h_buf[1, j], h_buf[2, j]
        if j > 0:
            hx_z, hy_z = h_buf[0, j - 1], h_buf[1, j - 1]
        else:
            hx_z, hy_z = kz_in[0] * keep_z, kz_in[1] * keep_z

        def down_x(v, i):
            edge = kx_in[i * depth + j : i * depth + j + 1, :] * keep_x
            return v - jnp.where(row == 0, edge, pltpu.roll(v, 1, 0))

        def down_y(v, i):
            edge = column(y_packed, i * depth + j, 0)
            return v - jnp.where(lane == 0, edge, pltpu.roll(v, 1, 1))

        side = (
            down_y(hz, 1) - (hy - hy_z),
            (hx - hx_z) - down_x(hz, 1),
            down_x(hy, 0) - down_y(hx, 0),
        )
        m = m_buf[j]
        decay, drive, coef = chosen(0, m), chosen(1, m), chosen(2, m)
        for i in range(3):
            e, pole = e_buf[i, j], p_buf[i, j]
            after = decay * pole + drive * e
            p_out[i, j] = after
            e_out[i, j] = e + coef * (side[i] - 0.5 * (after + pole))
            h_out[i, j] = h_buf[i, j]

    summed = total[pl.ds(pl.multiple_of(gz * rows, rows), rows), :]
    for copy in spread:
        copy.wait_recv()
    for k in range(n_gz - 1):
        summed = summed + from_gz[k]
    chunk[...] = summed

    def to_top():
        return send(
            chunk, top_in.at[pl.ds(pl.multiple_of(gz * rows, rows), rows)], top_send.at[0],
            top_recv.at[gz], {"gz": n_gz - 1},
        )

    @pl.when(jnp.logical_not(is_top))
    def _():
        to_top().start()

    def edge_x(kind):
        r = ((kind * 4 + 3) * half) % rows + half - 8
        return send(
            chunk.at[r : r + 8], bound_x.at[kind], bx_send.at[kind], bx_recv.at[kind],
            {"gx": step("gx", 1), "gz": n_gz - 1},
        )

    def edge_y(kind):
        r = ((kind * 4 + 2) * half) % rows
        return send(
            chunk.at[r : r + half], bound_y.at[kind], by_send.at[kind], by_recv.at[kind],
            {"gy": step("gy", 1), "gz": n_gz - 1},
        )

    for kind in range(2):
        @pl.when(gz == owner(kind, 3))
        def _():
            edge_x(kind).start()

        @pl.when(gz == owner(kind, 2))
        def _():
            edge_y(kind).start()

    @pl.when(is_top)
    def _():
        top_in[(n_gz - 1) * rows : n_gz * rows] = chunk[...]
        for k in range(n_gz - 1):
            send(
                chunk, top_in.at[k * rows : (k + 1) * rows], top_send.at[0], top_recv.at[k],
                {"gz": 0},
            ).wait_recv()
        for kind in range(2):
            edge_x(kind).wait_recv()
            edge_y(kind).wait_recv()

        def unfold(even, odd, at_row):
            lower = even - odd
            for j in range(half):
                low[at_row, half - 1 - j : half - j, :] = lower[j : j + 1, :]
            return jnp.concatenate([low[at_row], even + odd], axis=0)

        src = [
            unfold(
                top_in[c * half : (c + 1) * half, :],
                top_in[(4 + c) * half : (5 + c) * half, :],
                c,
            )
            for c in range(4)
        ]
        near_y = unfold(bound_y[0], bound_y[1], 4) * keep_y
        near_x = (bound_x[0, 7:8, :] + bound_x[1, 7:8, :]) * keep_x
        last = depth - 1
        coef = chosen(2, m_buf[last])
        h_out[0, last] = h_out[0, last] - COURANT * src[2]
        h_out[1, last] = h_out[1, last] - COURANT * src[3]
        behind_x = src[3] - jnp.where(row == 0, near_x, pltpu.roll(src[3], 1, 0))
        behind_y = src[2] - jnp.where(lane == 0, pltpu.roll(near_y, 1, 1), pltpu.roll(src[2], 1, 1))
        e_out[0, last] = e_out[0, last] + coef * (COURANT * src[3] - src[0])
        e_out[1, last] = e_out[1, last] - coef * (COURANT * src[2] + src[1])
        e_out[2, last] = e_out[2, last] - coef * (COURANT * (behind_x - behind_y))

    for copy in first + second + halo + halo2 + spread:
        copy.wait_send()
    for k in range(1, n_x):
        to_x(k).wait_send()

    @pl.when(jnp.logical_not(is_top))
    def _():
        to_top().wait_send()

    for kind in range(2):
        @pl.when(gz == owner(kind, 3))
        def _():
            edge_x(kind).wait_send()

        @pl.when(gz == owner(kind, 2))
        def _():
            edge_y(kind).wait_send()


def local(
    sizes, e_field, h_field, pole_current, material, pole_table, cotangent, cosines, wavenumber,
    time_phase,
):
    n_lo, n_hi, n_x, n_gz = sizes
    n_z = n_lo * n_hi
    depth, width_x, width_y = material.shape
    half = width_x // 2
    rows = 8 * half // n_gz
    block = (3, depth, width_x, width_y)
    vmem = pl.BlockSpec(memory_space=pltpu.VMEM)
    hbm = pl.BlockSpec(memory_space=pl.ANY)
    dma = pltpu.SemaphoreType.DMA
    cot = jnp.transpose(cotangent, (1, 2, 0))
    field = jax.ShapeDtypeStruct(block, F32)
    return tuple(
        pl.pallas_call(
            functools.partial(kernel, sizes),
            out_shape=(field, field, field),
            in_specs=[hbm] * 9,
            out_specs=(vmem, vmem, vmem),
            scratch_shapes=[
                pltpu.VMEM((8, 8, 16), F32),
                pltpu.SMEM((2, 8), F32),
                pltpu.SMEM((16,), F32),
                pltpu.SMEM((16,), F32),
                pltpu.SMEM((3, 4), F32),
                pltpu.VMEM(block, F32),
                pltpu.VMEM(block, F32),
                pltpu.VMEM(block, F32),
                pltpu.VMEM((depth, width_x, width_y), jnp.int32),
                pltpu.VMEM((n_lo, n_hi, 16, 128), F32),
                pltpu.VMEM((n_z, 2, half, 128), F32),
                pltpu.VMEM((n_x, n_z, 8, 128), F32),
                pltpu.VMEM((256, n_z * 256), BF16),
                pltpu.VMEM((256, n_z * 256), BF16),
                pltpu.VMEM((n_x - 1, 128, 128), F32),
                pltpu.VMEM((128, 128), F32),
                pltpu.VMEM((n_x - 1, 128, 128), F32),
                pltpu.VMEM((n_gz - 1, rows, 128), F32),
                pltpu.VMEM((rows, 128), F32),
                pltpu.VMEM((128, 128), F32),
                pltpu.VMEM((2, 8, 128), F32),
                pltpu.VMEM((2, half, 128), F32),
                pltpu.VMEM((5, half, 128), F32),
                pltpu.VMEM((8, 128), F32),
                pltpu.VMEM((8, 128), F32),
                pltpu.VMEM((8, 128), F32),
                pltpu.VMEM((8, 128), F32),
                pltpu.VMEM((2, width_x, 128), F32),
                pltpu.VMEM((8, 128), F32),
                pltpu.VMEM((8, 128), F32),
                pltpu.VMEM((8, 128), F32),
                pltpu.VMEM((8, 128), F32),
                pltpu.VMEM((2, width_x, 128), F32),
                dma((9,)),
                dma((6,)),
                dma((6,)),
                dma((n_x - 1,)),
                dma((n_x - 1,)),
                dma((n_gz - 1,)),
                dma((n_gz - 1,)),
                dma((1,)),
                dma((n_gz,)),
                dma((2,)),
                dma((2,)),
                dma((2,)),
                dma((2,)),
                dma((6,)),
                dma((6,)),
            ],
            compiler_params=pltpu.CompilerParams(
                collective_id=0, has_side_effects=True, vmem_limit_bytes=60 * 1024 * 1024
            ),
        )(cot, cosines, wavenumber, time_phase, pole_table, e_field, h_field, pole_current, material)
    )


def solution(mesh):
    sizes = (mesh.shape["gx"], PLANES, mesh.shape["gy"] // PLANES, mesh.shape["gz"])
    field = P(None, "gz", "gx", "gy")
    in_specs = (
        field,
        field,
        field,
        P("gz", "gx", "gy"),
        P(),
        P(None, None, ("gx", "gy", "gz")),
        P(None, ("gx", "gy", "gz")),
        P(),
        P(),
    )
    return jax.shard_map(
        functools.partial(local, sizes),
        mesh=mesh,
        in_specs=in_specs,
        out_specs=(field, field, field),
        check_vma=False,
    )
```

time: 228 us -> 50.9 us (0.22)
  the two profiles are of different devices: /device:TPU:11 before, /device:TPU:25 now
where the time goes in v1:
time: 50.9 us; the launch traced here: 50.7 us
  Pallas kernels  46.7 us (92%)
  local copies, waits for them, and re-layouts  3.33 us (7%)
  between operations  0.65 us (1%)
    pallas_call x1, Pallas kernels, local(): pl.pallas_call(functools.partial(kernel, sizes), out_shape=(field, field,...  46.7 us
    unnamed x7, local copies, waits for them, and re-layouts  3.33 us

profile of v1, /device:TPU:25, one launch (start us, length us, event | category | flops | bytes accessed | tf_op | source)
XLA Modules:
  0.0 50.7 jit_solution(3732275772935347213)
XLA Ops:
  0.6 46.7 %shard_map.112 = (f32[3,4,32,128]{3,2,1,0:T(8,128)}, f32[3,4,32,128]{3,2,1,0:T(8,128)}, f32[3,4,32,128]{3,2,1,0:T(8,128)}) custom-call(f32[8,8,16]{2,1,0:T(8,128)} %bitcast.1, f32[2,8]{1,0:T(2,128)} %cosines_in.1, f32[16]{0:T(128)} %wave_in.1, f32[16]{0:T(128)} %phase_in.1, f32[3,4]{1,0:T(4,128)} %table_in.1, f32[3,4,32,128]{3,2,1,0:T(8,128)} %e_in.1, ...), custom_call_target="tpu_custom_call" | custom-call | tf_op jit(solution)/shard_map/pallas_call | solution.py:528
  47.4 0.0 copy-start.1
  47.4 1.7 %copy.15 = f32[3,4,32,128]{3,2,1,0:T(8,128)} copy(f32[3,4,32,128]{3,2,1,0:T(8,128)} %get-tuple-element.6) | data formatting | bytes 393216
  49.0 0.0 copy-done.1
  49.0 0.0 copy-start
  49.0 0.7 %copy.16 = f32[3,4,32,128]{3,2,1,0:T(8,128)} copy(f32[3,4,32,128]{3,2,1,0:T(8,128)S(1)} %copy-done.1) | data formatting | bytes 393216
  49.7 0.3 copy-done
  50.0 0.7 %copy.17 = f32[3,4,32,128]{3,2,1,0:T(8,128)} copy(f32[3,4,32,128]{3,2,1,0:T(8,128)S(1)} %copy-done) | data formatting | bytes 393216
Async XLA Ops:
  47.4 1.7 %copy-start.1 = (f32[3,4,32,128]{3,2,1,0:T(8,128)S(1)}, f32[3,4,32,128]{3,2,1,0:T(8,128)}, u32[]{:S(2)}) copy-start(f32[3,4,32,128]{3,2,1,0:T(8,128)} %get-tuple-element.7) | copy-start | bytes 589828
  49.0 1.0 %copy-start = (f32[3,4,32,128]{3,2,1,0:T(8,128)S(1)}, f32[3,4,32,128]{3,2,1,0:T(8,128)}, u32[]{:S(2)}) copy-start(f32[3,4,32,128]{3,2,1,0:T(8,128)} %get-tuple-element.8) | copy-start | bytes 589828

commit v2 on v1

v2 whole, which is shorter than its diff:
```python
import functools
import math

import jax
import jax.numpy as jnp
from jax import lax
from jax.experimental import pallas as pl
from jax.experimental.pallas import tpu as pltpu
from jax.sharding import PartitionSpec as P

PLANES = 4
COURANT = 0.5
MESH = pl.DeviceIdType.MESH
F32 = jnp.float32
BF16 = jnp.bfloat16

TURN = 2.0 * math.pi
TURN_HI = 6.28125
TURN_LO = TURN - TURN_HI


def sincos(phase):
    turns = jnp.floor(phase * (1.0 / TURN) + 0.5)
    rest = ((phase - turns * TURN_HI) - turns * TURN_LO) * 0.25
    sq = rest * rest
    sin = rest + rest * sq * (
        -1.6666654611e-1 + sq * (8.3321608736e-3 + sq * -1.9515295891e-4)
    )
    cos = 1.0 - 0.5 * sq + sq * sq * (
        4.166664568298827e-2 + sq * (-1.388731625493765e-3 + sq * 2.443315711809948e-5)
    )
    for _ in range(2):
        sin, cos = 2.0 * sin * cos, 1.0 - 2.0 * sin * sin
    return sin, cos


def times(a, b):
    return a[0] * b[0] - a[1] * b[1], a[0] * b[1] + a[1] * b[0]


def split(value):
    high = value.astype(BF16)
    return high, (value - high.astype(F32)).astype(BF16)


def iota(shape, dim):
    return lax.broadcasted_iota(jnp.int32, shape, dim)


def kernel(
    sizes, cot_in, cosines_in, wave_in, phase_in, table_in, e_in, h_in, p_in, m_in,
    e_out, h_out, p_out, cot, cosines, wave, phase, table, e_buf, h_buf, p_buf, m_buf,
    gat, xs, edge, pq, yt, lt, acc, from_x, total, from_gz, low,
    hx_out, hx_in, hy_out, hy_in, hz_in, kx_out, kx_in, ky_out, ky_in, kz_in,
    load_sem, gat_send, gat_recv, x_send, x_recv, gz_send, gz_recv, halo_send, halo_recv,
):
    n_lo, n_hi, n_x, n_gz = sizes
    n_z = n_lo * n_hi
    n_half = n_z // 2
    depth, width_x, width_y = m_buf.shape
    half = width_x // 2
    gx, gy, gz = lax.axis_index("gx"), lax.axis_index("gy"), lax.axis_index("gz")
    z_hi = gy & (n_hi - 1)
    x = gy // n_hi
    z = z_hi * n_lo + gx
    is_top = gz == n_gz - 1

    def plane(other):
        return {"gx": other & (n_lo - 1), "gy": x * n_hi + other // n_lo}

    def column_of(k):
        return {"gy": ((x + k) & (n_x - 1)) * n_hi + z_hi}

    def copy_to(src, dst, send_sem, recv_sem, device):
        return pltpu.make_async_remote_copy(
            src_ref=src, dst_ref=dst, send_sem=send_sem, recv_sem=recv_sem,
            device_id=device, device_id_type=MESH,
        )

    loads = [
        pltpu.make_async_copy(a, b, load_sem.at[i])
        for i, (a, b) in enumerate(
            (
                (cot_in, cot),
                (cosines_in, cosines),
                (wave_in, wave),
                (phase_in, phase),
                (e_in, e_buf),
                (h_in, h_buf),
                (p_in, p_buf),
                (m_in, m_buf),
                (table_in, table),
            )
        )
    ]
    for load in loads:
        load.start()

    wrap_low = jnp.logical_and(z_hi == n_hi - 1, x < n_x - 1)
    wrap_high = jnp.logical_and(z_hi == 0, x > 0)

    barrier = pltpu.get_barrier_semaphore()

    def greet(device):
        pl.semaphore_signal(barrier, inc=1, device_id=device, device_id_type=MESH)

    def greet_plane(other, carry):
        greet(plane(other))
        return carry

    lax.fori_loop(z + 1, n_z, greet_plane, 0)
    for k in range(1, n_x):
        greet(column_of(k))

    @pl.when(gz < n_gz - 1)
    def _():
        greet({"gz": gz + 1})

    @pl.when(is_top)
    def _():
        for k in range(n_gz - 1):
            greet({"gz": k})

    @pl.when(wrap_high)
    def _():
        greet({"gy": gy - 1})

    greeted = (
        z
        + (n_x - 1)
        + (gz > 0).astype(jnp.int32)
        + (gz < n_gz - 1).astype(jnp.int32)
        + wrap_low.astype(jnp.int32)
    )

    for load in loads[:4]:
        load.wait()
    row8 = iota((8, 128), 0)
    lane8 = iota((8, 128), 1)
    lane1 = iota((1, 128), 1)
    freq = lane1 & 15
    direction = lane1 >> 4
    waves = jnp.zeros((1, 128), F32)
    delays = jnp.zeros((1, 128), F32)
    cos_x = jnp.zeros((1, 128), F32)
    cos_y = jnp.zeros((1, 128), F32)
    for f in range(16):
        waves = jnp.where(freq == f, wave[f], waves)
        delays = jnp.where(freq == f, phase[f], delays)
    for d in range(8):
        cos_x = jnp.where(direction == d, cosines[0, d], cos_x)
        cos_y = jnp.where(direction == d, cosines[1, d], cos_y)
    weights = jnp.concatenate([cot[:, d, :] for d in range(8)], axis=1)
    scale = 1.0 / math.sqrt(16.0 * 8 * n_lo * n_hi * n_x * n_gz)
    sin_t, cos_t = sincos(-delays)
    re = [weights[2 * c : 2 * c + 1] * scale for c in range(4)]
    im = [weights[2 * c + 1 : 2 * c + 2] * scale for c in range(4)]
    mine = gat.at[z]
    for c in range(4):
        mine[c : c + 1, :] = re[c] * cos_t - im[c] * sin_t
        mine[4 + c : 5 + c, :] = re[c] * sin_t + im[c] * cos_t
    mine[8:9, :] = waves * cos_x
    mine[9:10, :] = waves * cos_y

    pl.semaphore_wait(barrier, greeted)

    def share(other):
        block = gat.at[z, 0:10]
        return copy_to(block, block, gat_send.at[other], gat_recv.at[z], plane(other))

    def arrival(other):
        block = gat.at[other, 0:10]
        return copy_to(block, block, gat_send.at[other], gat_recv.at[other], plane(other))

    def share_down(other, carry):
        share(other).start()
        return carry

    lax.fori_loop(0, z, share_down, 0)

    loads[4].wait()
    groups = width_x // 8
    low_x, high_x = gx > 0, gx < n_lo - 1
    low_z, high_z = gz > 0, gz < n_gz - 1
    low_y, high_y = gy > 0, gy < n_hi * n_x - 1
    plain_low_y, plain_high_y = z_hi > 0, z_hi < n_hi - 1
    ex_copy = copy_to(hx_out, hx_in, halo_send.at[0], halo_recv.at[0], {"gx": gx - 1})
    ey_copy = copy_to(hy_out, hy_in, halo_send.at[1], halo_recv.at[1], {"gy": gy - 1})
    ez_copy = copy_to(
        e_buf.at[0:2, 0], hz_in, halo_send.at[2], halo_recv.at[2], {"gz": gz - 1}
    )
    hx_copy = copy_to(kx_out, kx_in, halo_send.at[3], halo_recv.at[3], {"gx": gx + 1})
    hy_copy = copy_to(ky_out, ky_in, halo_send.at[4], halo_recv.at[4], {"gy": gy + 1})
    hz_copy = copy_to(
        h_buf.at[0:2, depth - 1], kz_in, halo_send.at[5], halo_recv.at[5], {"gz": gz + 1}
    )

    def when(flag, action):
        @pl.when(flag)
        def _():
            action()

    when(low_z, ez_copy.start)
    for i in range(2):
        for j in range(depth):
            hx_out[i * depth + j : i * depth + j + 1, :] = e_buf[1 + i, j, 0:1, :]
    when(low_x, ex_copy.start)
    packed = jnp.zeros((8, 128), F32)
    for i in range(2):
        for j in range(depth):
            for g in range(groups):
                to = (i * depth + j) * groups + g
                col = e_buf[2 * i, j, 8 * g : 8 * g + 8, :]
                packed = jnp.where(lane8 == to, pltpu.roll(col, to, 1) if to else col, packed)
    hy_out[...] = packed
    when(plain_low_y, ey_copy.start)

    loads[5].wait()
    when(high_x, ex_copy.wait_recv)
    when(plain_high_y, ey_copy.wait_recv)
    when(high_z, ez_copy.wait_recv)
    row = iota((width_x, 128), 0)
    lane = iota((width_x, 128), 1)

    def column(packed, which, lane_to):
        cols = []
        for g in range(groups):
            by = (lane_to - which * groups - g) % 128
            cols.append(pltpu.roll(packed, by, 1) if by else packed)
        return jnp.concatenate(cols, axis=0)

    x_edges = jnp.where(high_x, hx_in[...], 0.0)
    y_packed = jnp.where(plain_high_y, hy_in[...], 0.0)
    z_edges = [jnp.where(high_z, hz_in[i], 0.0) for i in range(2)]
    for j in range(depth):
        ex, ey, ez = e_buf[0, j], e_buf[1, j], e_buf[2, j]
        ex_z, ey_z = (e_buf[0, j + 1], e_buf[1, j + 1]) if j < depth - 1 else z_edges

        def up_x(v, i):
            next_row = x_edges[i * depth + j : i * depth + j + 1, :]
            return jnp.where(row == width_x - 1, next_row, pltpu.roll(v, width_x - 1, 0)) - v

        def up_y(v, i):
            next_col = column(y_packed, i * depth + j, 127)
            return jnp.where(lane == 127, next_col, pltpu.roll(v, 127, 1)) - v

        h_buf[0, j] = h_buf[0, j] - COURANT * (up_y(ez, 1) - (ey_z - ey))
        h_buf[1, j] = h_buf[1, j] - COURANT * ((ex_z - ex) - up_x(ez, 1))
        h_buf[2, j] = h_buf[2, j] - COURANT * (up_x(ey, 0) - up_y(ex, 0))

    packed = jnp.zeros((8, 128), F32)
    for i in range(2):
        for j in range(depth):
            for g in range(groups):
                to = (i * depth + j) * groups + g
                col = h_buf[2 * i, j, 8 * g : 8 * g + 8, :]
                packed = jnp.where(lane8 == to, pltpu.roll(col, to + 1, 1), packed)
    ky_out[...] = packed
    when(high_y, hy_copy.start)

    def send_hx_hz():
        for i in range(2):
            for j in range(depth):
                kx_out[i * depth + j : i * depth + j + 1, :] = h_buf[
                    1 + i, j, width_x - 1 : width_x, :
                ]
        when(high_x, hx_copy.start)
        when(high_z, hz_copy.start)

    when(jnp.logical_not(wrap_low), send_hx_hz)

    def collect(first):
        def one(i, carry):
            other = first + i

            @pl.when(other != z)
            def _():
                arrival(other).wait_recv()

            @pl.when(other > z)
            def _():
                share(other).start()

            return carry

        lax.fori_loop(0, n_half, one, 0)

    rowf = row8.astype(F32)
    centre = (gx * width_x).astype(F32) + (0.5 * width_x - 0.5)
    tile_y = ((row8 * n_hi + z_hi) * width_y).astype(F32)
    mul_x = jnp.where(
        row8 < 4, centre, jnp.where(row8 == 5, half + 0.5, jnp.where(row8 == 7, 8.0, 0.0))
    )
    mul_y = jnp.where(
        row8 < 4, tile_y, jnp.where(row8 == 4, 8.0, jnp.where(row8 == 6, 64.0, 0.0))
    )
    sign = jnp.where(row8 < 4, -1.0, 1.0)

    def factors_of(first):
        def factors(s, carry):
            along_x = gat[first + s, 8:9, :]
            along_y = gat[first + s, 9:10, :]
            w = gat[first + s, 0:8, :]
            turned = pltpu.roll(w, 4, 0) * sign
            sin_m, cos_m = sincos(along_x * mul_x + along_y * mul_y)
            for t in range(n_x):
                pq[t, s] = w * cos_m[t : t + 1] + turned * sin_m[t : t + 1]
            sin_b, cos_b = sincos(along_x * (rowf + 0.5))
            more = times((cos_b, sin_b), (cos_m[7:8], sin_m[7:8]))
            xs[s, 0, 0:8] = cos_b
            xs[s, 0, 8:16] = more[0]
            xs[s, 1, 0:8] = sin_b
            xs[s, 1, 8:16] = more[1]
            edge[s, 0:1] = cos_m[5:6]
            edge[s, 1:2] = -sin_m[5:6]
            sin_b, cos_b = sincos(along_y * rowf)
            edge[s, 2:3] = cos_b[1:2]
            edge[s, 3:4] = -sin_b[1:2]
            e8 = (cos_m[4:5], sin_m[4:5])
            e16 = times(e8, e8)
            more = times((cos_b, sin_b), e8)
            block = (jnp.concatenate([cos_b, more[0]], 0), jnp.concatenate([sin_b, more[1]], 0))
            blocks = [block]
            for power in (e16, times(e16, e16), (cos_m[6:7], sin_m[6:7])):
                blocks = blocks + [times(b, power) for b in blocks]
            for g, b in enumerate(blocks):
                for kind in range(2):
                    high, lowp = split(b[kind])
                    base = pl.multiple_of(s * 256 + kind * 128, 128)
                    yt[16 * g : 16 * g + 16, pl.ds(base, 128)] = high
                    yt[128 + 16 * g : 144 + 16 * g, pl.ds(base, 128)] = lowp
            return carry

        lax.fori_loop(0, n_half, factors, 0)

    row16 = iota((16, 128), 0)
    lane16 = iota((16, 128), 1)

    def tile(t):
        def build(s, cols):
            cx, sx = xs[s, 0], xs[s, 1]
            nx = -sx

            def put(r, k, value):
                high, lowp = split(value)
                base = pl.multiple_of(s * 256 + k * 128, 128)
                lt[r : r + 16, pl.ds(base, 128)] = high
                lt[144 + r : 160 + r, pl.ds(base, 128)] = lowp

            for c in range(4):
                p = pq[t, s, c : c + 1, :]
                nq = -pq[t, s, 4 + c : 5 + c, :]
                products = ((p * cx, nq * cx), (nq * sx, p * nx))
                for kind in range(2):
                    for k in range(2):
                        put((kind * 4 + c) * half, k, products[kind][k])
                if c == 2:
                    cy, sy = edge[s, 2:3, :], edge[s, 3:4, :]
                    cols = tuple(
                        old + (new[0] * cy + new[1] * sy) for old, new in zip(cols, products)
                    )
                if c == 3:
                    ox, oy = edge[s, 0:1, :], edge[s, 1:2, :]
                    put(128, 0, jnp.broadcast_to(p * ox + nq * oy, (16, 128)))
                    put(128, 1, jnp.broadcast_to(nq * ox - p * oy, (16, 128)))
            return cols

        zero = jnp.zeros((16, 128), F32)
        cols = lax.fori_loop(0, n_half, build, (zero, zero))
        both = lax.dot_general(
            lt[...], yt[...], (((1,), (1,)), ((), ())), preferred_element_type=F32
        )
        main = both[0:136, 0:128] + (both[0:136, 128:256] + both[144:280, 0:128])
        before = jnp.zeros((1, 128), F32)
        for kind in range(2):
            sums = jnp.sum(cols[kind], axis=1, keepdims=True)
            placed = jnp.where(lane16 == row16 + 16 * kind, sums, 0.0)
            before = before + jnp.sum(placed, axis=0, keepdims=True)
        return main[0:128], jnp.where(row8 == 0, main[128:136], jnp.where(row8 == 1, before, 0.0))

    own_half = (z // n_half) * n_half
    other_half = n_half - own_half
    collect(own_half)
    factors_of(own_half)

    def first_pass(k, carry):
        main, rest = tile((x + k) & (n_x - 1))
        acc[k, 0:128] = main
        acc[k, 128:136] = rest
        return carry

    lax.fori_loop(0, n_x, first_pass, 0)
    collect(other_half)

    @pl.when(wrap_high)
    def _():
        hy_copy.wait_recv()
        ey_copy.start()

    factors_of(other_half)

    def to_x(k):
        return copy_to(
            acc.at[k], from_x.at[k - 1], x_send.at[k - 1], x_recv.at[k - 1], column_of(k)
        )

    def second_pass(i, carry):
        k = jnp.where(i == n_x - 1, 0, jnp.where(i == 0, n_x // 2, jnp.where(i == 1, 1, i + 1)))
        main, rest = tile((x + k) & (n_x - 1))
        acc[k, 0:128] = acc[k, 0:128] + main
        acc[k, 128:136] = acc[k, 128:136] + rest

        @pl.when(k > 0)
        def _():
            to_x(k).start()

        return carry

    lax.fori_loop(0, n_x, second_pass, 0)

    @pl.when(wrap_low)
    def _():
        ey_copy.wait_recv()
        late = hy_in[...]
        for j in range(depth):
            h_buf[0, j] = h_buf[0, j] - jnp.where(
                lane == 127, COURANT * column(late, depth + j, 127), 0.0
            )
            h_buf[2, j] = h_buf[2, j] + jnp.where(
                lane == 127, COURANT * column(late, j, 127), 0.0
            )
        send_hx_hz()

    for load in loads[6:]:
        load.wait()
    when(low_x, hx_copy.wait_recv)
    when(plain_low_y, hy_copy.wait_recv)
    when(low_z, hz_copy.wait_recv)
    x_edges = jnp.where(low_x, kx_in[...], 0.0)
    y_packed = jnp.where(low_y, ky_in[...], 0.0)
    z_edges = [jnp.where(low_z, kz_in[i], 0.0) for i in range(2)]
    missing = jnp.where(wrap_high, COURANT, 0.0)

    def chosen(which, m):
        value = jnp.full(m.shape, table[which, 3], F32)
        for i in range(3):
            value = jnp.where(m == i, table[which, i], value)
        return value

    for j in range(depth):
        hx, hy, hz = h_buf[0, j], h_buf[1, j], h_buf[2, j]
        hx_z, hy_z = (h_buf[0, j - 1], h_buf[1, j - 1]) if j > 0 else z_edges
        ex, ey, ez = e_buf[0, j], e_buf[1, j], e_buf[2, j]

        def down_x(v, i):
            last_row = x_edges[i * depth + j : i * depth + j + 1, :]
            return v - jnp.where(row == 0, last_row, pltpu.roll(v, 1, 0))

        def down_y(v, i, rest):
            last_col = column(y_packed, i * depth + j, 0) + rest
            return v - jnp.where(lane == 0, last_col, pltpu.roll(v, 1, 1))

        side = (
            down_y(hz, 1, missing * ex) - (hy - hy_z),
            (hx - hx_z) - down_x(hz, 1),
            down_x(hy, 0) - down_y(hx, 0, -missing * ez),
        )
        m = m_buf[j]
        decay, drive, coef = chosen(0, m), chosen(1, m), chosen(2, m)
        for i, e in enumerate((ex, ey, ez)):
            pole = p_buf[i, j]
            after = decay * pole + drive * e
            p_out[i, j] = after
            e_out[i, j] = e + coef * (side[i] - 0.5 * (after + pole))
            h_out[i, j] = h_buf[i, j]

    for k in range(1, n_x):
        to_x(k).wait_recv()
    total[...] = sum((from_x[k] for k in range(n_x - 1)), acc[0])

    def to_top(k):
        return copy_to(
            total, from_gz.at[k], gz_send.at[0], gz_recv.at[k], {"gz": n_gz - 1}
        )

    @pl.when(jnp.logical_not(is_top))
    def _():
        to_top(gz).start()

    @pl.when(is_top)
    def _():
        for k in range(n_gz - 1):
            copy_to(
                total, from_gz.at[k], gz_send.at[0], gz_recv.at[k], {"gz": 0}
            ).wait_recv()
        summed = sum((from_gz[k] for k in range(n_gz - 1)), total[...])

        def unfold(even, odd, spot):
            lower = even - odd
            for j in range(half):
                low[spot, half - 1 - j : half - j, :] = lower[j : j + 1, :]
            return jnp.concatenate([low[spot], even + odd], axis=0)

        src = [
            unfold(
                summed[c * half : (c + 1) * half], summed[(4 + c) * half : (5 + c) * half], c
            )
            for c in range(4)
        ]
        near_x = jnp.where(low_x, summed[128:129], 0.0)
        before = jnp.where(low_y, summed[129:130], 0.0)
        sides = [
            jnp.broadcast_to(
                jnp.sum(
                    jnp.where(lane16 == row16 + 16 * kind, before, 0.0), axis=1, keepdims=True
                ),
                (16, 128),
            )
            for kind in range(2)
        ]
        near_y = unfold(sides[0], sides[1], 4)
        last = depth - 1
        coef = chosen(2, m_buf[last])
        h_out[0, last] = h_out[0, last] - COURANT * src[2]
        h_out[1, last] = h_out[1, last] - COURANT * src[3]
        behind_x = src[3] - jnp.where(row == 0, near_x, pltpu.roll(src[3], 1, 0))
        behind_y = src[2] - jnp.where(lane == 0, near_y, pltpu.roll(src[2], 1, 1))
        e_out[0, last] = e_out[0, last] + coef * (COURANT * src[3] - src[0])
        e_out[1, last] = e_out[1, last] - coef * (COURANT * src[2] + src[1])
        e_out[2, last] = e_out[2, last] - coef * (COURANT * (behind_x - behind_y))

    def sent(other, carry):
        @pl.when(other != z)
        def _():
            share(other).wait_send()

        return carry

    lax.fori_loop(0, n_z, sent, 0)
    for k in range(1, n_x):
        to_x(k).wait_send()
    when(low_x, ex_copy.wait_send)
    when(low_y, ey_copy.wait_send)
    when(low_z, ez_copy.wait_send)
    when(high_x, hx_copy.wait_send)
    when(high_y, hy_copy.wait_send)
    when(high_z, hz_copy.wait_send)
    when(jnp.logical_not(is_top), to_top(gz).wait_send)


def local(
    sizes, e_field, h_field, pole_current, material, pole_table, cotangent, cosines, wavenumber,
    time_phase,
):
    n_lo, n_hi, n_x, n_gz = sizes
    n_z = n_lo * n_hi
    depth, width_x, width_y = material.shape
    half = width_x // 2
    block = (3, depth, width_x, width_y)
    vmem = pl.BlockSpec(memory_space=pltpu.VMEM)
    hbm = pl.BlockSpec(memory_space=pl.ANY)
    dma = pltpu.SemaphoreType.DMA
    cot = jnp.transpose(cotangent, (1, 2, 0))
    field = jax.ShapeDtypeStruct(block, F32)
    return tuple(
        pl.pallas_call(
            functools.partial(kernel, sizes),
            out_shape=(field, field, field),
            in_specs=[hbm] * 9,
            out_specs=(vmem, vmem, vmem),
            scratch_shapes=[
                pltpu.VMEM((8, 8, 16), F32),
                pltpu.SMEM((2, 8), F32),
                pltpu.SMEM((16,), F32),
                pltpu.SMEM((16,), F32),
                pltpu.SMEM((3, 4), F32),
                pltpu.VMEM(block, F32),
                pltpu.VMEM(block, F32),
                pltpu.VMEM(block, F32),
                pltpu.VMEM((depth, width_x, width_y), jnp.int32),
                pltpu.VMEM((n_z, 16, 128), F32),
                pltpu.VMEM((n_z // 2, 2, half, 128), F32),
                pltpu.VMEM((n_z // 2, 8, 128), F32),
                pltpu.VMEM((n_x, n_z // 2, 8, 128), F32),
                pltpu.VMEM((256, n_z * 128), BF16),
                pltpu.VMEM((288, n_z * 128), BF16),
                pltpu.VMEM((n_x, 136, 128), F32),
                pltpu.VMEM((n_x - 1, 136, 128), F32),
                pltpu.VMEM((136, 128), F32),
                pltpu.VMEM((n_gz - 1, 136, 128), F32),
                pltpu.VMEM((5, half, 128), F32),
                pltpu.VMEM((8, 128), F32),
                pltpu.VMEM((8, 128), F32),
                pltpu.VMEM((8, 128), F32),
                pltpu.VMEM((8, 128), F32),
                pltpu.VMEM((2, width_x, 128), F32),
                pltpu.VMEM((8, 128), F32),
                pltpu.VMEM((8, 128), F32),
                pltpu.VMEM((8, 128), F32),
                pltpu.VMEM((8, 128), F32),
                pltpu.VMEM((2, width_x, 128), F32),
                dma((9,)),
                dma((n_z,)),
                dma((n_z,)),
                dma((n_x - 1,)),
                dma((n_x - 1,)),
                dma((1,)),
                dma((n_gz - 1,)),
                dma((6,)),
                dma((6,)),
            ],
            compiler_params=pltpu.CompilerParams(
                collective_id=0, has_side_effects=True, vmem_limit_bytes=60 * 1024 * 1024
            ),
        )(cot, cosines, wavenumber, time_phase, pole_table, e_field, h_field, pole_current, material)
    )


def solution(mesh):
    sizes = (mesh.shape["gx"], PLANES, mesh.shape["gy"] // PLANES, mesh.shape["gz"])
    field = P(None, "gz", "gx", "gy")
    in_specs = (
        field,
        field,
        field,
        P("gz", "gx", "gy"),
        P(),
        P(None, None, ("gx", "gy", "gz")),
        P(None, ("gx", "gy", "gz")),
        P(),
        P(),
    )
    return jax.shard_map(
        functools.partial(local, sizes),
        mesh=mesh,
        in_specs=in_specs,
        out_specs=(field, field, field),
        check_vma=False,
    )
```

time: 50.9 us -> 52.3 us (1.028)
  the two profiles are of different devices: /device:TPU:25 before, /device:TPU:505 now
where the time goes in v2:
time: 52.3 us; the launch traced here: 52.1 us
  Pallas kernels  48.2 us (92%)
  local copies, waits for them, and re-layouts  3.33 us (6%)
  between operations  0.65 us (1%)
    pallas_call x1, Pallas kernels, local(): pl.pallas_call(functools.partial(kernel, sizes), out_shape=(field, field,...  48.2 us
    unnamed x7, local copies, waits for them, and re-layouts  3.33 us

profile of v2, /device:TPU:505, one launch (start us, length us, event | category | flops | bytes accessed | tf_op | source)
XLA Modules:
  0.0 52.1 jit_solution(15099831370088634286)
XLA Ops:
  0.6 48.2 %shard_map.112 = (f32[3,4,32,128]{3,2,1,0:T(8,128)}, f32[3,4,32,128]{3,2,1,0:T(8,128)}, f32[3,4,32,128]{3,2,1,0:T(8,128)}) custom-call(f32[8,8,16]{2,1,0:T(8,128)} %bitcast.1, f32[2,8]{1,0:T(2,128)} %cosines_in.1, f32[16]{0:T(128)} %wave_in.1, f32[16]{0:T(128)} %phase_in.1, f32[3,4]{1,0:T(4,128)} %table_in.1, f32[3,4,32,128]{3,2,1,0:T(8,128)} %e_in.1, ...), custom_call_target="tpu_custom_call" | custom-call | tf_op jit(solution)/shard_map/pallas_call | solution.py:566
  48.8 0.0 copy-start.1
  48.8 1.7 %copy.15 = f32[3,4,32,128]{3,2,1,0:T(8,128)} copy(f32[3,4,32,128]{3,2,1,0:T(8,128)} %get-tuple-element.6) | data formatting | bytes 393216
  50.5 0.0 copy-done.1
  50.5 0.0 copy-start
  50.5 0.7 %copy.16 = f32[3,4,32,128]{3,2,1,0:T(8,128)} copy(f32[3,4,32,128]{3,2,1,0:T(8,128)S(1)} %copy-done.1) | data formatting | bytes 393216
  51.2 0.3 copy-done
  51.5 0.7 %copy.17 = f32[3,4,32,128]{3,2,1,0:T(8,128)} copy(f32[3,4,32,128]{3,2,1,0:T(8,128)S(1)} %copy-done) | data formatting | bytes 393216
Async XLA Ops:
  48.8 1.7 %copy-start.1 = (f32[3,4,32,128]{3,2,1,0:T(8,128)S(1)}, f32[3,4,32,128]{3,2,1,0:T(8,128)}, u32[]{:S(2)}) copy-start(f32[3,4,32,128]{3,2,1,0:T(8,128)} %get-tuple-element.7) | copy-start | bytes 589828
  50.5 1.0 %copy-start = (f32[3,4,32,128]{3,2,1,0:T(8,128)S(1)}, f32[3,4,32,128]{3,2,1,0:T(8,128)}, u32[]{:S(2)}) copy-start(f32[3,4,32,128]{3,2,1,0:T(8,128)} %get-tuple-element.8) | copy-start | bytes 589828

commit v3 on v2

--- a/solution.py
+++ b/solution.py
@@ -53,6 +53,7 @@
     gat, xs, edge, pq, yt, lt, acc, from_x, total, from_gz, low,
     hx_out, hx_in, hy_out, hy_in, hz_in, kx_out, kx_in, ky_out, ky_in, kz_in,
     load_sem, gat_send, gat_recv, x_send, x_recv, gz_send, gz_recv, halo_send, halo_recv,
+    x_token, top_token,
 ):
     n_lo, n_hi, n_x, n_gz = sizes
     n_z = n_lo * n_hi
@@ -109,17 +110,20 @@
         return carry
 
     lax.fori_loop(z + 1, n_z, greet_plane, 0)
-    for k in range(1, n_x):
-        greet(column_of(k))
+
+    def greet_column(other, carry):
+        greet({"gy": other * n_hi + z_hi})
+        return carry
+
+    lax.fori_loop(x + 1, n_x, greet_column, 0)
 
     @pl.when(gz < n_gz - 1)
     def _():
         greet({"gz": gz + 1})
 
-    @pl.when(is_top)
-    def _():
-        for k in range(n_gz - 1):
-            greet({"gz": k})
+    @pl.when(gz < n_gz - 2)
+    def _():
+        greet({"gz": n_gz - 1})
 
     @pl.when(wrap_high)
     def _():
@@ -127,9 +131,8 @@
 
     greeted = (
         z
-        + (n_x - 1)
-        + (gz > 0).astype(jnp.int32)
-        + (gz < n_gz - 1).astype(jnp.int32)
+        + x
+        + jnp.where(is_top, n_gz - 1, (gz > 0).astype(jnp.int32))
         + wrap_low.astype(jnp.int32)
     )
 
@@ -162,7 +165,9 @@
     mine[8:9, :] = waves * cos_x
     mine[9:10, :] = waves * cos_y
 
-    pl.semaphore_wait(barrier, greeted)
+    @pl.when(greeted > 0)
+    def _():
+        pl.semaphore_wait(barrier, greeted)
 
     def share(other):
         block = gat.at[z, 0:10]
@@ -177,6 +182,19 @@
         return carry
 
     lax.fori_loop(0, z, share_down, 0)
+
+    def tell_column(other, carry):
+        pl.semaphore_signal(
+            x_token, inc=1, device_id={"gy": other * n_hi + z_hi}, device_id_type=MESH
+        )
+        return carry
+
+    lax.fori_loop(0, x, tell_column, 0)
+
+    @pl.when(is_top)
+    def _():
+        for k in range(n_gz - 1):
+            pl.semaphore_signal(top_token, inc=1, device_id={"gz": k}, device_id_type=MESH)
 
     loads[4].wait()
     groups = width_x // 8
@@ -215,67 +233,25 @@
     hy_out[...] = packed
     when(plain_low_y, ey_copy.start)
 
-    loads[5].wait()
-    when(high_x, ex_copy.wait_recv)
-    when(plain_high_y, ey_copy.wait_recv)
-    when(high_z, ez_copy.wait_recv)
-    row = iota((width_x, 128), 0)
-    lane = iota((width_x, 128), 1)
-
-    def column(packed, which, lane_to):
-        cols = []
-        for g in range(groups):
-            by = (lane_to - which * groups - g) % 128
-            cols.append(pltpu.roll(packed, by, 1) if by else packed)
-        return jnp.concatenate(cols, axis=0)
-
-    x_edges = jnp.where(high_x, hx_in[...], 0.0)
-    y_packed = jnp.where(plain_high_y, hy_in[...], 0.0)
-    z_edges = [jnp.where(high_z, hz_in[i], 0.0) for i in range(2)]
-    for j in range(depth):
-        ex, ey, ez = e_buf[0, j], e_buf[1, j], e_buf[2, j]
-        ex_z, ey_z = (e_buf[0, j + 1], e_buf[1, j + 1]) if j < depth - 1 else z_edges
-
-        def up_x(v, i):
-            next_row = x_edges[i * depth + j : i * depth + j + 1, :]
-            return jnp.where(row == width_x - 1, next_row, pltpu.roll(v, width_x - 1, 0)) - v
-
-        def up_y(v, i):
-            next_col = column(y_packed, i * depth + j, 127)
-            return jnp.where(lane == 127, next_col, pltpu.roll(v, 127, 1)) - v
-
-        h_buf[0, j] = h_buf[0, j] - COURANT * (up_y(ez, 1) - (ey_z - ey))
-        h_buf[1, j] = h_buf[1, j] - COURANT * ((ex_z - ex) - up_x(ez, 1))
-        h_buf[2, j] = h_buf[2, j] - COURANT * (up_x(ey, 0) - up_y(ex, 0))
-
-    packed = jnp.zeros((8, 128), F32)
-    for i in range(2):
-        for j in range(depth):
-            for g in range(groups):
-                to = (i * depth + j) * groups + g
-                col = h_buf[2 * i, j, 8 * g : 8 * g + 8, :]
-                packed = jnp.where(lane8 == to, pltpu.roll(col, to + 1, 1), packed)
-    ky_out[...] = packed
-    when(high_y, hy_copy.start)
-
-    def send_hx_hz():
-        for i in range(2):
-            for j in range(depth):
-                kx_out[i * depth + j : i * depth + j + 1, :] = h_buf[
-                    1 + i, j, width_x - 1 : width_x, :
-                ]
-        when(high_x, hx_copy.start)
-        when(high_z, hz_copy.start)
-
-    when(jnp.logical_not(wrap_low), send_hx_hz)
-
-    def collect(first):
+    def wait_for(other, carry):
+        arrival(other).wait_recv()
+        return carry
+
+    def answer(other, carry):
+        arrival(other).wait_recv()
+        share(other).start()
+        return carry
+
+    def collect_own(first):
+        lax.fori_loop(z + 1, first + n_half, answer, 0)
+        lax.fori_loop(first, z, wait_for, 0)
+
+    def collect_other(first):
+        near_first = (z & (n_half - 1)) < n_half // 2
+
         def one(i, carry):
-            other = first + i
-
-            @pl.when(other != z)
-            def _():
-                arrival(other).wait_recv()
+            other = jnp.where(near_first, first + (n_half - 1) - i, first + i)
+            arrival(other).wait_recv()
 
             @pl.when(other > z)
             def _():
@@ -380,7 +356,7 @@
 
     own_half = (z // n_half) * n_half
     other_half = n_half - own_half
-    collect(own_half)
+    collect_own(own_half)
     factors_of(own_half)
 
     def first_pass(k, carry):
@@ -390,12 +366,62 @@
         return carry
 
     lax.fori_loop(0, n_x, first_pass, 0)
-    collect(other_half)
-
-    @pl.when(wrap_high)
-    def _():
-        hy_copy.wait_recv()
-        ey_copy.start()
+
+    loads[5].wait()
+    when(high_x, ex_copy.wait_recv)
+    when(plain_high_y, ey_copy.wait_recv)
+    when(high_z, ez_copy.wait_recv)
+    row = iota((width_x, 128), 0)
+    lane = iota((width_x, 128), 1)
+
+    def column(packed, which, lane_to):
+        cols = []
+        for g in range(groups):
+            by = (lane_to - which * groups - g) % 128
+            cols.append(pltpu.roll(packed, by, 1) if by else packed)
+        return jnp.concatenate(cols, axis=0)
+
+    x_edges = jnp.where(high_x, hx_in[...], 0.0)
+    y_packed = jnp.where(plain_high_y, hy_in[...], 0.0)
+    z_edges = [jnp.where(high_z, hz_in[i], 0.0) for i in range(2)]
+    for j in range(depth):
+        ex, ey, ez = e_buf[0, j], e_buf[1, j], e_buf[2, j]
+        ex_z, ey_z = (e_buf[0, j + 1], e_buf[1, j + 1]) if j < depth - 1 else z_edges
+
+        def up_x(v, i):
+            next_row = x_edges[i * depth + j : i * depth + j + 1, :]
+            return jnp.where(row == width_x - 1, next_row, pltpu.roll(v, width_x - 1, 0)) - v
+
+        def up_y(v, i):
+            next_col = column(y_packed, i * depth + j, 127)
+            return jnp.where(lane == 127, next_col, pltpu.roll(v, 127, 1)) - v
+
+        h_buf[0, j] = h_buf[0, j] - COURANT * (up_y(ez, 1) - (ey_z - ey))
+        h_buf[1, j] = h_buf[1, j] - COURANT * ((ex_z - ex) - up_x(ez, 1))
+        h_buf[2, j] = h_buf[2, j] - COURANT * (up_x(ey, 0) - up_y(ex, 0))
+
+    packed = jnp.zeros((8, 128), F32)
+    for i in range(2):
+        for j in range(depth):
+            for g in range(groups):
+                to = (i * depth + j) * groups + g
+                col = h_buf[2 * i, j, 8 * g : 8 * g + 8, :]
+                packed = jnp.where(lane8 == to, pltpu.roll(col, to + 1, 1), packed)
+    ky_out[...] = packed
+    when(high_y, hy_copy.start)
+
+    def send_hx_hz():
+        for i in range(2):
+            for j in range(depth):
+                kx_out[i * depth + j : i * depth + j + 1, :] = h_buf[
+                    1 + i, j, width_x - 1 : width_x, :
+                ]
+        when(high_x, hx_copy.start)
+        when(high_z, hz_copy.start)
+
+    when(jnp.logical_not(wrap_low), send_hx_hz)
+
+    collect_other(other_half)
 
     factors_of(other_half)
 
@@ -403,6 +429,10 @@
         return copy_to(
             acc.at[k], from_x.at[k - 1], x_send.at[k - 1], x_recv.at[k - 1], column_of(k)
         )
+
+    @pl.when(x < n_x - 1)
+    def _():
+        pl.semaphore_wait(x_token, n_x - 1 - x)
 
     def second_pass(i, carry):
         k = jnp.where(i == n_x - 1, 0, jnp.where(i == 0, n_x // 2, jnp.where(i == 1, 1, i + 1)))
@@ -417,6 +447,11 @@
         return carry
 
     lax.fori_loop(0, n_x, second_pass, 0)
+
+    @pl.when(wrap_high)
+    def _():
+        hy_copy.wait_recv()
+        ey_copy.start()
 
     @pl.when(wrap_low)
     def _():
@@ -485,6 +520,7 @@
 
     @pl.when(jnp.logical_not(is_top))
     def _():
+        pl.semaphore_wait(top_token, 1)
         to_top(gz).start()
 
     @pl.when(is_top)
@@ -548,6 +584,11 @@
     when(jnp.logical_not(is_top), to_top(gz).wait_send)
 
 
+def put(*refs):
+    for src, dst in zip(refs[:3], refs[3:]):
+        dst[...] = src[...]
+
+
 def local(
     sizes, e_field, h_field, pole_current, material, pole_table, cotangent, cosines, wavenumber,
     time_phase,
@@ -562,57 +603,66 @@
     dma = pltpu.SemaphoreType.DMA
     cot = jnp.transpose(cotangent, (1, 2, 0))
     field = jax.ShapeDtypeStruct(block, F32)
+    results = pl.pallas_call(
+        functools.partial(kernel, sizes),
+        out_shape=(field, field, field),
+        in_specs=[hbm] * 9,
+        out_specs=(vmem, vmem, vmem),
+        scratch_shapes=[
+            pltpu.VMEM((8, 8, 16), F32),
+            pltpu.SMEM((2, 8), F32),
+            pltpu.SMEM((16,), F32),
+            pltpu.SMEM((16,), F32),
+            pltpu.SMEM((3, 4), F32),
+            pltpu.VMEM(block, F32),
+            pltpu.VMEM(block, F32),
+            pltpu.VMEM(block, F32),
+            pltpu.VMEM((depth, width_x, width_y), jnp.int32),
+            pltpu.VMEM((n_z, 16, 128), F32),
+            pltpu.VMEM((n_z // 2, 2, half, 128), F32),
+            pltpu.VMEM((n_z // 2, 8, 128), F32),
+            pltpu.VMEM((n_x, n_z // 2, 8, 128), F32),
+            pltpu.VMEM((256, n_z * 128), BF16),
+            pltpu.VMEM((288, n_z * 128), BF16),
+            pltpu.VMEM((n_x, 136, 128), F32),
+            pltpu.VMEM((n_x - 1, 136, 128), F32),
+            pltpu.VMEM((136, 128), F32),
+            pltpu.VMEM((n_gz - 1, 136, 128), F32),
+            pltpu.VMEM((5, half, 128), F32),
+            pltpu.VMEM((8, 128), F32),
+            pltpu.VMEM((8, 128), F32),
+            pltpu.VMEM((8, 128), F32),
+            pltpu.VMEM((8, 128), F32),
+            pltpu.VMEM((2, width_x, 128), F32),
+            pltpu.VMEM((8, 128), F32),
+            pltpu.VMEM((8, 128), F32),
+            pltpu.VMEM((8, 128), F32),
+            pltpu.VMEM((8, 128), F32),
+            pltpu.VMEM((2, width_x, 128), F32),
+            dma((9,)),
+            dma((n_z,)),
+            dma((n_z,)),
+            dma((n_x - 1,)),
+            dma((n_x - 1,)),
+            dma((1,)),
+            dma((n_gz - 1,)),
+            dma((6,)),
+            dma((6,)),
+            pltpu.SemaphoreType.REGULAR,
+            pltpu.SemaphoreType.REGULAR,
+        ],
+        compiler_params=pltpu.CompilerParams(
+            collective_id=0, has_side_effects=True, vmem_limit_bytes=60 * 1024 * 1024
+        ),
+    )(cot, cosines, wavenumber, time_phase, pole_table, e_field, h_field, pole_current, material)
     return tuple(
         pl.pallas_call(
-            functools.partial(kernel, sizes),
+            put,
             out_shape=(field, field, field),
-            in_specs=[hbm] * 9,
-            out_specs=(vmem, vmem, vmem),
-            scratch_shapes=[
-                pltpu.VMEM((8, 8, 16), F32),
-                pltpu.SMEM((2, 8), F32),
-                pltpu.SMEM((16,), F32),
-                pltpu.SMEM((16,), F32),
-                pltpu.SMEM((3, 4), F32),
-                pltpu.VMEM(block, F32),
-                pltpu.VMEM(block, F32),
-                pltpu.VMEM(block, F32),
-                pltpu.VMEM((depth, width_x, width_y), jnp.int32),
-                pltpu.VMEM((n_z, 16, 128), F32),
-                pltpu.VMEM((n_z // 2, 2, half, 128), F32),
-                pltpu.VMEM((n_z // 2, 8, 128), F32),
-                pltpu.VMEM((n_x, n_z // 2, 8, 128), F32),
-                pltpu.VMEM((256, n_z * 128), BF16),
-                pltpu.VMEM((288, n_z * 128), BF16),
-                pltpu.VMEM((n_x, 136, 128), F32),
-                pltpu.VMEM((n_x - 1, 136, 128), F32),
-                pltpu.VMEM((136, 128), F32),
-                pltpu.VMEM((n_gz - 1, 136, 128), F32),
-                pltpu.VMEM((5, half, 128), F32),
-                pltpu.VMEM((8, 128), F32),
-                pltpu.VMEM((8, 128), F32),
-                pltpu.VMEM((8, 128), F32),
-                pltpu.VMEM((8, 128), F32),
-                pltpu.VMEM((2, width_x, 128), F32),
-                pltpu.VMEM((8, 128), F32),
-                pltpu.VMEM((8, 128), F32),
-                pltpu.VMEM((8, 128), F32),
-                pltpu.VMEM((8, 128), F32),
-                pltpu.VMEM((2, width_x, 128), F32),
-                dma((9,)),
-                dma((n_z,)),
-                dma((n_z,)),
-                dma((n_x - 1,)),
-                dma((n_x - 1,)),
-                dma((1,)),
-                dma((n_gz - 1,)),
-                dma((6,)),
-                dma((6,)),
-            ],
-            compiler_params=pltpu.CompilerParams(
-                collective_id=0, has_side_effects=True, vmem_limit_bytes=60 * 1024 * 1024
-            ),
-        )(cot, cosines, wavenumber, time_phase, pole_table, e_field, h_field, pole_current, material)
+            in_specs=[vmem] * 3,
+            out_specs=(vmem,) * 3,
+            compiler_params=pltpu.CompilerParams(vmem_limit_bytes=60 * 1024 * 1024),
+        )(*results)
     )
 
 

time: 52.3 us -> 42 us (0.80)
  the two profiles are of different devices: /device:TPU:505 before, /device:TPU:509 now
where the time goes in v3:
time: 42 us; the launch traced here: 41.8 us
  Pallas kernels  41.2 us (98%)
  between operations  0.64 us (2%)
    pallas_call x1, Pallas kernels, local(): pl.pallas_call(functools.partial(kernel, sizes), out_shape=(field, field,...  39.2 us
    pallas_call x1, Pallas kernels, local(): pl.pallas_call(put, out_shape=(field, field, field), in_specs=[vmem] * 3,...  1.94 us

profile of v3, /device:TPU:509, one launch (start us, length us, event | category | flops | bytes accessed | tf_op | source)
XLA Modules:
  0.0 41.8 jit_solution(8797471642109793114)
XLA Ops:
  0.6 39.2 %shard_map.112 = (f32[3,4,32,128]{3,2,1,0:T(8,128)}, f32[3,4,32,128]{3,2,1,0:T(8,128)}, f32[3,4,32,128]{3,2,1,0:T(8,128)}) custom-call(f32[8,8,16]{2,1,0:T(8,128)} %bitcast.1, f32[2,8]{1,0:T(2,128)} %cosines_in.1, f32[16]{0:T(128)} %wave_in.1, f32[16]{0:T(128)} %phase_in.1, f32[3,4]{1,0:T(4,128)} %table_in.1, f32[3,4,32,128]{3,2,1,0:T(8,128)} %e_in.1, ...), custom_call_target="tpu_custom_call" | custom-call | tf_op jit(solution)/shard_map/pallas_call | solution.py:606
  39.9 1.9 %shard_map.113 = (f32[3,4,32,128]{3,2,1,0:T(8,128)}, f32[3,4,32,128]{3,2,1,0:T(8,128)}, f32[3,4,32,128]{3,2,1,0:T(8,128)}) custom-call(f32[3,4,32,128]{3,2,1,0:T(8,128)} %get-tuple-element.6.refs_0_, f32[3,4,32,128]{3,2,1,0:T(8,128)} %get-tuple-element.7.refs_1_, f32[3,4,32,128]{3,2,1,0:T(8,128)} %get-tuple-element.8.refs_2_), custom_call_target="tpu_custom_call" | custom-call | tf_op jit(solution)/shard_map/pallas_call | solution.py:659

commit v4 on v3

--- a/solution.py
+++ b/solution.py
@@ -50,7 +50,7 @@
 def kernel(
     sizes, cot_in, cosines_in, wave_in, phase_in, table_in, e_in, h_in, p_in, m_in,
     e_out, h_out, p_out, cot, cosines, wave, phase, table, e_buf, h_buf, p_buf, m_buf,
-    gat, xs, edge, pq, yt, lt, acc, from_x, total, from_gz, low,
+    gat, yt, lt, cols, acc, from_x, total, from_gz, low,
     hx_out, hx_in, hy_out, hy_in, hz_in, kx_out, kx_in, ky_out, ky_in, kz_in,
     load_sem, gat_send, gat_recv, x_send, x_recv, gz_send, gz_recv, halo_send, halo_recv,
     x_token, top_token,
@@ -63,10 +63,15 @@
     gx, gy, gz = lax.axis_index("gx"), lax.axis_index("gy"), lax.axis_index("gz")
     z_hi = gy & (n_hi - 1)
     x = gy // n_hi
-    z = z_hi * n_lo + gx
+    def swap(k):
+        return jnp.where(k < n_half, k, n_z + n_half - 1 - k)
+
+    z = swap(z_hi * n_lo + gx)
+    is_late = z >= n_half
     is_top = gz == n_gz - 1
 
     def plane(other):
+        other = swap(other)
         return {"gx": other & (n_lo - 1), "gy": x * n_hi + other // n_lo}
 
     def column_of(k):
@@ -129,8 +134,18 @@
     def _():
         greet({"gy": gy - 1})
 
+    @pl.when(jnp.logical_and(is_late, gx < n_lo - 1))
+    def _():
+        greet({"gx": gx + 1})
+
+    @pl.when(jnp.logical_and(is_late, z_hi < n_hi - 1))
+    def _():
+        greet({"gy": gy + 1})
+
     greeted = (
-        z
+        jnp.logical_and(is_late, gx > 0).astype(jnp.int32)
+        + (z_hi > n_hi // 2).astype(jnp.int32)
+        + z
         + x
         + jnp.where(is_top, n_gz - 1, (gz > 0).astype(jnp.int32))
         + wrap_low.astype(jnp.int32)
@@ -233,144 +248,6 @@
     hy_out[...] = packed
     when(plain_low_y, ey_copy.start)
 
-    def wait_for(other, carry):
-        arrival(other).wait_recv()
-        return carry
-
-    def answer(other, carry):
-        arrival(other).wait_recv()
-        share(other).start()
-        return carry
-
-    def collect_own(first):
-        lax.fori_loop(z + 1, first + n_half, answer, 0)
-        lax.fori_loop(first, z, wait_for, 0)
-
-    def collect_other(first):
-        near_first = (z & (n_half - 1)) < n_half // 2
-
-        def one(i, carry):
-            other = jnp.where(near_first, first + (n_half - 1) - i, first + i)
-            arrival(other).wait_recv()
-
-            @pl.when(other > z)
-            def _():
-                share(other).start()
-
-            return carry
-
-        lax.fori_loop(0, n_half, one, 0)
-
-    rowf = row8.astype(F32)
-    centre = (gx * width_x).astype(F32) + (0.5 * width_x - 0.5)
-    tile_y = ((row8 * n_hi + z_hi) * width_y).astype(F32)
-    mul_x = jnp.where(
-        row8 < 4, centre, jnp.where(row8 == 5, half + 0.5, jnp.where(row8 == 7, 8.0, 0.0))
-    )
-    mul_y = jnp.where(
-        row8 < 4, tile_y, jnp.where(row8 == 4, 8.0, jnp.where(row8 == 6, 64.0, 0.0))
-    )
-    sign = jnp.where(row8 < 4, -1.0, 1.0)
-
-    def factors_of(first):
-        def factors(s, carry):
-            along_x = gat[first + s, 8:9, :]
-            along_y = gat[first + s, 9:10, :]
-            w = gat[first + s, 0:8, :]
-            turned = pltpu.roll(w, 4, 0) * sign
-            sin_m, cos_m = sincos(along_x * mul_x + along_y * mul_y)
-            for t in range(n_x):
-                pq[t, s] = w * cos_m[t : t + 1] + turned * sin_m[t : t + 1]
-            sin_b, cos_b = sincos(along_x * (rowf + 0.5))
-            more = times((cos_b, sin_b), (cos_m[7:8], sin_m[7:8]))
-            xs[s, 0, 0:8] = cos_b
-            xs[s, 0, 8:16] = more[0]
-            xs[s, 1, 0:8] = sin_b
-            xs[s, 1, 8:16] = more[1]
-            edge[s, 0:1] = cos_m[5:6]
-            edge[s, 1:2] = -sin_m[5:6]
-            sin_b, cos_b = sincos(along_y * rowf)
-            edge[s, 2:3] = cos_b[1:2]
-            edge[s, 3:4] = -sin_b[1:2]
-            e8 = (cos_m[4:5], sin_m[4:5])
-            e16 = times(e8, e8)
-            more = times((cos_b, sin_b), e8)
-            block = (jnp.concatenate([cos_b, more[0]], 0), jnp.concatenate([sin_b, more[1]], 0))
-            blocks = [block]
-            for power in (e16, times(e16, e16), (cos_m[6:7], sin_m[6:7])):
-                blocks = blocks + [times(b, power) for b in blocks]
-            for g, b in enumerate(blocks):
-                for kind in range(2):
-                    high, lowp = split(b[kind])
-                    base = pl.multiple_of(s * 256 + kind * 128, 128)
-                    yt[16 * g : 16 * g + 16, pl.ds(base, 128)] = high
-                    yt[128 + 16 * g : 144 + 16 * g, pl.ds(base, 128)] = lowp
-            return carry
-
-        lax.fori_loop(0, n_half, factors, 0)
-
-    row16 = iota((16, 128), 0)
-    lane16 = iota((16, 128), 1)
-
-    def tile(t):
-        def build(s, cols):
-            cx, sx = xs[s, 0], xs[s, 1]
-            nx = -sx
-
-            def put(r, k, value):
-                high, lowp = split(value)
-                base = pl.multiple_of(s * 256 + k * 128, 128)
-                lt[r : r + 16, pl.ds(base, 128)] = high
-                lt[144 + r : 160 + r, pl.ds(base, 128)] = lowp
-
-            for c in range(4):
-                p = pq[t, s, c : c + 1, :]
-                nq = -pq[t, s, 4 + c : 5 + c, :]
-                products = ((p * cx, nq * cx), (nq * sx, p * nx))
-                for kind in range(2):
-                    for k in range(2):
-                        put((kind * 4 + c) * half, k, products[kind][k])
-                if c == 2:
-                    cy, sy = edge[s, 2:3, :], edge[s, 3:4, :]
-                    cols = tuple(
-                        old + (new[0] * cy + new[1] * sy) for old, new in zip(cols, products)
-                    )
-                if c == 3:
-                    ox, oy = edge[s, 0:1, :], edge[s, 1:2, :]
-                    put(128, 0, jnp.broadcast_to(p * ox + nq * oy, (16, 128)))
-                    put(128, 1, jnp.broadcast_to(nq * ox - p * oy, (16, 128)))
-            return cols
-
-        zero = jnp.zeros((16, 128), F32)
-        cols = lax.fori_loop(0, n_half, build, (zero, zero))
-        both = lax.dot_general(
-            lt[...], yt[...], (((1,), (1,)), ((), ())), preferred_element_type=F32
-        )
-        main = both[0:136, 0:128] + (both[0:136, 128:256] + both[144:280, 0:128])
-        before = jnp.zeros((1, 128), F32)
-        for kind in range(2):
-            sums = jnp.sum(cols[kind], axis=1, keepdims=True)
-            placed = jnp.where(lane16 == row16 + 16 * kind, sums, 0.0)
-            before = before + jnp.sum(placed, axis=0, keepdims=True)
-        return main[0:128], jnp.where(row8 == 0, main[128:136], jnp.where(row8 == 1, before, 0.0))
-
-    own_half = (z // n_half) * n_half
-    other_half = n_half - own_half
-    collect_own(own_half)
-    factors_of(own_half)
-
-    def first_pass(k, carry):
-        main, rest = tile((x + k) & (n_x - 1))
-        acc[k, 0:128] = main
-        acc[k, 128:136] = rest
-        return carry
-
-    lax.fori_loop(0, n_x, first_pass, 0)
-
-    loads[5].wait()
-    when(high_x, ex_copy.wait_recv)
-    when(plain_high_y, ey_copy.wait_recv)
-    when(high_z, ez_copy.wait_recv)
     row = iota((width_x, 128), 0)
     lane = iota((width_x, 128), 1)
 
@@ -380,35 +257,6 @@
             by = (lane_to - which * groups - g) % 128
             cols.append(pltpu.roll(packed, by, 1) if by else packed)
         return jnp.concatenate(cols, axis=0)
-
-    x_edges = jnp.where(high_x, hx_in[...], 0.0)
-    y_packed = jnp.where(plain_high_y, hy_in[...], 0.0)
-    z_edges = [jnp.where(high_z, hz_in[i], 0.0) for i in range(2)]
-    for j in range(depth):
-        ex, ey, ez = e_buf[0, j], e_buf[1, j], e_buf[2, j]
-        ex_z, ey_z = (e_buf[0, j + 1], e_buf[1, j + 1]) if j < depth - 1 else z_edges
-
-        def up_x(v, i):
-            next_row = x_edges[i * depth + j : i * depth + j + 1, :]
-            return jnp.where(row == width_x - 1, next_row, pltpu.roll(v, width_x - 1, 0)) - v
-
-        def up_y(v, i):
-            next_col = column(y_packed, i * depth + j, 127)
-            return jnp.where(lane == 127, next_col, pltpu.roll(v, 127, 1)) - v
-
-        h_buf[0, j] = h_buf[0, j] - COURANT * (up_y(ez, 1) - (ey_z - ey))
-        h_buf[1, j] = h_buf[1, j] - COURANT * ((ex_z - ex) - up_x(ez, 1))
-        h_buf[2, j] = h_buf[2, j] - COURANT * (up_x(ey, 0) - up_y(ex, 0))
-
-    packed = jnp.zeros((8, 128), F32)
-    for i in range(2):
-        for j in range(depth):
-            for g in range(groups):
-                to = (i * depth + j) * groups + g
-                col = h_buf[2 * i, j, 8 * g : 8 * g + 8, :]
-                packed = jnp.where(lane8 == to, pltpu.roll(col, to + 1, 1), packed)
-    ky_out[...] = packed
-    when(high_y, hy_copy.start)
 
     def send_hx_hz():
         for i in range(2):
@@ -419,11 +267,182 @@
         when(high_x, hx_copy.start)
         when(high_z, hz_copy.start)
 
-    when(jnp.logical_not(wrap_low), send_hx_hz)
-
-    collect_other(other_half)
-
-    factors_of(other_half)
+    def magnetic():
+        loads[5].wait()
+        when(high_x, ex_copy.wait_recv)
+        when(plain_high_y, ey_copy.wait_recv)
+        when(high_z, ez_copy.wait_recv)
+        x_edges = jnp.where(high_x, hx_in[...], 0.0)
+        y_packed = jnp.where(plain_high_y, hy_in[...], 0.0)
+        z_edges = [jnp.where(high_z, hz_in[i], 0.0) for i in range(2)]
+        for j in range(depth):
+            ex, ey, ez = e_buf[0, j], e_buf[1, j], e_buf[2, j]
+            ex_z, ey_z = (e_buf[0, j + 1], e_buf[1, j + 1]) if j < depth - 1 else z_edges
+
+            def up_x(v, i):
+                next_row = x_edges[i * depth + j : i * depth + j + 1, :]
+                return jnp.where(row == width_x - 1, next_row, pltpu.roll(v, width_x - 1, 0)) - v
+
+            def up_y(v, i):
+                next_col = column(y_packed, i * depth + j, 127)
+                return jnp.where(lane == 127, next_col, pltpu.roll(v, 127, 1)) - v
+
+            h_buf[0, j] = h_buf[0, j] - COURANT * (up_y(ez, 1) - (ey_z - ey))
+            h_buf[1, j] = h_buf[1, j] - COURANT * ((ex_z - ex) - up_x(ez, 1))
+            h_buf[2, j] = h_buf[2, j] - COURANT * (up_x(ey, 0) - up_y(ex, 0))
+
+        packed = jnp.zeros((8, 128), F32)
+        for i in range(2):
+            for j in range(depth):
+                for g in range(groups):
+                    to = (i * depth + j) * groups + g
+                    col = h_buf[2 * i, j, 8 * g : 8 * g + 8, :]
+                    packed = jnp.where(lane8 == to, pltpu.roll(col, to + 1, 1), packed)
+        ky_out[...] = packed
+        when(high_y, hy_copy.start)
+
+        when(jnp.logical_not(wrap_low), send_hx_hz)
+
+    when(is_late, magnetic)
+
+    rowf = row8.astype(F32)
+    centre = (gx * width_x).astype(F32) + (0.5 * width_x - 0.5)
+    tile_y = ((row8 * n_hi + z_hi) * width_y).astype(F32)
+    mul_x = jnp.where(
+        row8 < 4, centre, jnp.where(row8 == 5, half + 0.5, jnp.where(row8 == 7, 8.0, 0.0))
+    )
+    mul_y = jnp.where(
+        row8 < 4, tile_y, jnp.where(row8 == 4, 8.0, jnp.where(row8 == 6, 64.0, 0.0))
+    )
+    sign = jnp.where(row8 < 4, -1.0, 1.0)
+
+    row16 = iota((16, 128), 0)
+    lane16 = iota((16, 128), 1)
+
+    def operands(rank, s):
+        along_x = gat[rank, 8:9, :]
+        along_y = gat[rank, 9:10, :]
+        w = gat[rank, 0:8, :]
+        turned = pltpu.roll(w, 4, 0) * sign
+        sin_m, cos_m = sincos(along_x * mul_x + along_y * mul_y)
+
+        def spot(k):
+            return pl.ds(pl.multiple_of(s * 256 + k * 128, 128), 128)
+
+        sin_b, cos_b = sincos(along_y * rowf)
+        before_y = (cos_b[1:2], -sin_b[1:2])
+        e8 = (cos_m[4:5], sin_m[4:5])
+        e16 = times(e8, e8)
+        more = times((cos_b, sin_b), e8)
+        blocks = [(jnp.concatenate([cos_b, more[0]], 0), jnp.concatenate([sin_b, more[1]], 0))]
+        for power in (e16, times(e16, e16), (cos_m[6:7], sin_m[6:7])):
+            blocks = blocks + [times(b, power) for b in blocks]
+        for g, b in enumerate(blocks):
+            for kind in range(2):
+                high, lowp = split(b[kind])
+                yt[16 * g : 16 * g + 16, spot(kind)] = high
+                yt[128 + 16 * g : 144 + 16 * g, spot(kind)] = lowp
+
+        sin_b, cos_b = sincos(along_x * (rowf + 0.5))
+        more = times((cos_b, sin_b), (cos_m[7:8], sin_m[7:8]))
+        cx = jnp.concatenate([cos_b, more[0]], 0)
+        sx = jnp.concatenate([sin_b, more[1]], 0)
+        nx = -sx
+        before_x = (cos_m[5:6], -sin_m[5:6])
+        for t in range(n_x):
+            pq = w * cos_m[t : t + 1] + turned * sin_m[t : t + 1]
+
+            def put_left(r, k, value):
+                high, lowp = split(value)
+                lt[t, r : r + 16, spot(k)] = high
+                lt[t, 144 + r : 160 + r, spot(k)] = lowp
+
+            for c in range(4):
+                p = pq[c : c + 1, :]
+                nq = -pq[4 + c : 5 + c, :]
+                products = ((p * cx, nq * cx), (nq * sx, p * nx))
+                for kind in range(2):
+                    for k in range(2):
+                        put_left((kind * 4 + c) * half, k, products[kind][k])
+                if c == 2:
+                    for kind in range(2):
+                        cols[t, kind] = cols[t, kind] + (
+                            products[kind][0] * before_y[0] + products[kind][1] * before_y[1]
+                        )
+                if c == 3:
+                    ox, oy = before_x
+                    put_left(128, 0, jnp.broadcast_to(p * ox + nq * oy, (16, 128)))
+                    put_left(128, 1, jnp.broadcast_to(nq * ox - p * oy, (16, 128)))
+
+    def answer(other, carry):
+        arrival(other).wait_recv()
+        share(other).start()
+        return carry
+
+    def answer_late():
+        def one(i, carry):
+            return answer(jnp.where(is_far, n_z - 1 - i, n_half + i), carry)
+
+        lax.fori_loop(0, n_half, one, 0)
+
+    def own_planes(i, carry):
+        other = own_half + ((z + 1 + i) & (n_half - 1))
+
+        @pl.when(jnp.logical_or(other < z, jnp.logical_and(other > z, jnp.logical_not(is_far))))
+        def _():
+            arrival(other).wait_recv()
+
+        @pl.when(jnp.logical_and(other > z, jnp.logical_not(is_far)))
+        def _():
+            share(other).start()
+
+        operands(other, other - own_half)
+        return carry
+
+    def other_planes(i, carry):
+        @pl.when(is_late)
+        def _():
+            arrival(i).wait_recv()
+
+        operands(other_half + i, i)
+        return carry
+
+    def tile(t):
+        both = lax.dot_general(
+            lt[t], yt[...], (((1,), (1,)), ((), ())), preferred_element_type=F32
+        )
+        main = both[0:136, 0:128] + (both[0:136, 128:256] + both[144:280, 0:128])
+        before = jnp.zeros((1, 128), F32)
+        for kind in range(2):
+            sums = jnp.sum(cols[t, kind], axis=1, keepdims=True)
+            placed = jnp.where(lane16 == row16 + 16 * kind, sums, 0.0)
+            before = before + jnp.sum(placed, axis=0, keepdims=True)
+        cols[t] = jnp.zeros((2, 16, 128), F32)
+        return main[0:128], jnp.where(row8 == 0, main[128:136], jnp.where(row8 == 1, before, 0.0))
+
+    cols[...] = jnp.zeros(cols.shape, F32)
+    own_half = (z // n_half) * n_half
+    other_half = n_half - own_half
+    is_far = jnp.logical_and(z >= n_half // 2, jnp.logical_not(is_late))
+
+    @pl.when(is_far)
+    def _():
+        lax.fori_loop(z + 1, n_half, answer, 0)
+        answer_late()
+
+    lax.fori_loop(0, n_half, own_planes, 0)
+
+    def first_pass(k, carry):
+        main, rest = tile((x + k) & (n_x - 1))
+        acc[k, 0:128] = main
+        acc[k, 128:136] = rest
+        return carry
+
+    lax.fori_loop(0, n_x, first_pass, 0)
+
+    when(jnp.logical_not(is_late), magnetic)
+    when(z < n_half // 2, answer_late)
+    lax.fori_loop(0, n_half, other_planes, 0)
 
     def to_x(k):
         return copy_to(
@@ -465,6 +484,20 @@
                 lane == 127, COURANT * column(late, j, 127), 0.0
             )
         send_hx_hz()
+
+    for k in range(1, n_x):
+        to_x(k).wait_recv()
+    total[...] = sum((from_x[k] for k in range(n_x - 1)), acc[0])
+
+    def to_top(k):
+        return copy_to(
+            total, from_gz.at[k], gz_send.at[0], gz_recv.at[k], {"gz": n_gz - 1}
+        )
+
+    @pl.when(jnp.logical_not(is_top))
+    def _():
+        pl.semaphore_wait(top_token, 1)
+        to_top(gz).start()
 
     for load in loads[6:]:
         load.wait()
@@ -508,20 +541,6 @@
             p_out[i, j] = after
             e_out[i, j] = e + coef * (side[i] - 0.5 * (after + pole))
             h_out[i, j] = h_buf[i, j]
-
-    for k in range(1, n_x):
-        to_x(k).wait_recv()
-    total[...] = sum((from_x[k] for k in range(n_x - 1)), acc[0])
-
-    def to_top(k):
-        return copy_to(
-            total, from_gz.at[k], gz_send.at[0], gz_recv.at[k], {"gz": n_gz - 1}
-        )
-
-    @pl.when(jnp.logical_not(is_top))
-    def _():
-        pl.semaphore_wait(top_token, 1)
-        to_top(gz).start()
 
     @pl.when(is_top)
     def _():
@@ -619,11 +638,9 @@
             pltpu.VMEM(block, F32),
             pltpu.VMEM((depth, width_x, width_y), jnp.int32),
             pltpu.VMEM((n_z, 16, 128), F32),
-            pltpu.VMEM((n_z // 2, 2, half, 128), F32),
-            pltpu.VMEM((n_z // 2, 8, 128), F32),
-            pltpu.VMEM((n_x, n_z // 2, 8, 128), F32),
             pltpu.VMEM((256, n_z * 128), BF16),
-            pltpu.VMEM((288, n_z * 128), BF16),
+            pltpu.VMEM((n_x, 288, n_z * 128), BF16),
+            pltpu.VMEM((n_x, 2, half, 128), F32),
             pltpu.VMEM((n_x, 136, 128), F32),
             pltpu.VMEM((n_x - 1, 136, 128), F32),
             pltpu.VMEM((136, 128), F32),

time: 42 us -> 37.5 us (0.89)
  the two profiles are of different devices: /device:TPU:509 before, /device:TPU:153 now
where the time goes in v4:
time: 37.5 us; the launch traced here: 37.4 us
  Pallas kernels  36.7 us (98%)
  between operations  0.64 us (2%)
    pallas_call x1, Pallas kernels, local(): pl.pallas_call(functools.partial(kernel, sizes), out_shape=(field, field,...  34.8 us
    pallas_call x1, Pallas kernels, local(): pl.pallas_call(put, out_shape=(field, field, field), in_specs=[vmem] * 3,...  1.94 us

profile of v4, /device:TPU:153, one launch (start us, length us, event | category | flops | bytes accessed | tf_op | source)
XLA Modules:
  0.0 37.4 jit_solution(13908368427795225306)
XLA Ops:
  0.6 34.8 %shard_map.112 = (f32[3,4,32,128]{3,2,1,0:T(8,128)}, f32[3,4,32,128]{3,2,1,0:T(8,128)}, f32[3,4,32,128]{3,2,1,0:T(8,128)}) custom-call(f32[8,8,16]{2,1,0:T(8,128)} %bitcast.1, f32[2,8]{1,0:T(2,128)} %cosines_in.1, f32[16]{0:T(128)} %wave_in.1, f32[16]{0:T(128)} %phase_in.1, f32[3,4]{1,0:T(4,128)} %table_in.1, f32[3,4,32,128]{3,2,1,0:T(8,128)} %e_in.1, ...), custom_call_target="tpu_custom_call" | custom-call | tf_op jit(solution)/shard_map/pallas_call | solution.py:625
  35.4 1.9 %shard_map.113 = (f32[3,4,32,128]{3,2,1,0:T(8,128)}, f32[3,4,32,128]{3,2,1,0:T(8,128)}, f32[3,4,32,128]{3,2,1,0:T(8,128)}) custom-call(f32[3,4,32,128]{3,2,1,0:T(8,128)} %get-tuple-element.6.refs_0_, f32[3,4,32,128]{3,2,1,0:T(8,128)} %get-tuple-element.7.refs_1_, f32[3,4,32,128]{3,2,1,0:T(8,128)} %get-tuple-element.8.refs_2_), custom_call_target="tpu_custom_call" | custom-call | tf_op jit(solution)/shard_map/pallas_call | solution.py:676

commit v5 on v4

--- a/solution.py
+++ b/solution.py
@@ -52,7 +52,7 @@
     e_out, h_out, p_out, cot, cosines, wave, phase, table, e_buf, h_buf, p_buf, m_buf,
     gat, yt, lt, cols, acc, from_x, total, from_gz, low,
     hx_out, hx_in, hy_out, hy_in, hz_in, kx_out, kx_in, ky_out, ky_in, kz_in,
-    load_sem, gat_send, gat_recv, x_send, x_recv, gz_send, gz_recv, halo_send, halo_recv,
+    load_sem, store_sem, gat_send, gat_recv, x_send, x_recv, gz_send, gz_recv, halo_send, halo_recv,
     x_token, top_token,
 ):
     n_lo, n_hi, n_x, n_gz = sizes
@@ -68,7 +68,10 @@
 
     z = swap(z_hi * n_lo + gx)
     is_late = z >= n_half
+    n_y = n_gz // 2
+    y, core = gz // 2, gz & 1
     is_top = gz == n_gz - 1
+    adds = core == 1
 
     def plane(other):
         other = swap(other)
@@ -117,7 +120,12 @@
     lax.fori_loop(z + 1, n_z, greet_plane, 0)
 
     def greet_column(other, carry):
-        greet({"gy": other * n_hi + z_hi})
+        greet({"gy": other * n_hi + z_hi, "gz": 2 * y + 1})
+
+        @pl.when(adds)
+        def _():
+            greet({"gy": other * n_hi + z_hi, "gz": 2 * y})
+
         return carry
 
     lax.fori_loop(x + 1, n_x, greet_column, 0)
@@ -126,7 +134,7 @@
     def _():
         greet({"gz": gz + 1})
 
-    @pl.when(gz < n_gz - 2)
+    @pl.when(jnp.logical_and(adds, gz < n_gz - 1))
     def _():
         greet({"gz": n_gz - 1})
 
@@ -146,8 +154,8 @@
         jnp.logical_and(is_late, gx > 0).astype(jnp.int32)
         + (z_hi > n_hi // 2).astype(jnp.int32)
         + z
-        + x
-        + jnp.where(is_top, n_gz - 1, (gz > 0).astype(jnp.int32))
+        + x * (1 + core)
+        + jnp.where(is_top, n_y, (gz > 0).astype(jnp.int32))
         + wrap_low.astype(jnp.int32)
     )
 
@@ -198,18 +206,23 @@
 
     lax.fori_loop(0, z, share_down, 0)
 
+    def tell(semaphore, device):
+        pl.semaphore_signal(semaphore, inc=1, device_id=device, device_id_type=MESH)
+
     def tell_column(other, carry):
-        pl.semaphore_signal(
-            x_token, inc=1, device_id={"gy": other * n_hi + z_hi}, device_id_type=MESH
-        )
-        return carry
-
-    lax.fori_loop(0, x, tell_column, 0)
+        for which in range(2):
+            tell(x_token, {"gy": other * n_hi + z_hi, "gz": 2 * y + which})
+        return carry
+
+    @pl.when(adds)
+    def _():
+        lax.fori_loop(0, x, tell_column, 0)
+        tell(x_token, {"gz": gz - 1})
 
     @pl.when(is_top)
     def _():
-        for k in range(n_gz - 1):
-            pl.semaphore_signal(top_token, inc=1, device_id={"gz": k}, device_id_type=MESH)
+        for k in range(n_y - 1):
+            tell(top_token, {"gz": 2 * k + 1})
 
     loads[4].wait()
     groups = width_x // 8
@@ -307,12 +320,19 @@
 
     rowf = row8.astype(F32)
     centre = (gx * width_x).astype(F32) + (0.5 * width_x - 0.5)
-    tile_y = ((row8 * n_hi + z_hi) * width_y).astype(F32)
+    n_a = n_x // 2
+    tile_y = ((row8 * (2 * n_hi) + z_hi) * width_y).astype(F32)
     mul_x = jnp.where(
-        row8 < 4, centre, jnp.where(row8 == 5, half + 0.5, jnp.where(row8 == 7, 8.0, 0.0))
+        row8 < 2, centre, jnp.where(row8 == 5, half + 0.5, jnp.where(row8 == 7, 8.0, 0.0))
     )
     mul_y = jnp.where(
-        row8 < 4, tile_y, jnp.where(row8 == 4, 8.0, jnp.where(row8 == 6, 64.0, 0.0))
+        row8 < 2,
+        tile_y,
+        jnp.where(
+            row8 == 2,
+            float(n_hi * width_y),
+            jnp.where(row8 == 4, 8.0, jnp.where(row8 == 6, 64.0, 0.0)),
+        ),
     )
     sign = jnp.where(row8 < 4, -1.0, 1.0)
 
@@ -330,18 +350,21 @@
             return pl.ds(pl.multiple_of(s * 256 + k * 128, 128), 128)
 
         sin_b, cos_b = sincos(along_y * rowf)
-        before_y = (cos_b[1:2], -sin_b[1:2])
+        run = (cos_m[2:3], sin_m[2:3])
+        before_y = [(cos_b[1:2], -sin_b[1:2])]
+        before_y.append(times(before_y[0], run))
         e8 = (cos_m[4:5], sin_m[4:5])
         e16 = times(e8, e8)
         more = times((cos_b, sin_b), e8)
         blocks = [(jnp.concatenate([cos_b, more[0]], 0), jnp.concatenate([sin_b, more[1]], 0))]
         for power in (e16, times(e16, e16), (cos_m[6:7], sin_m[6:7])):
             blocks = blocks + [times(b, power) for b in blocks]
-        for g, b in enumerate(blocks):
-            for kind in range(2):
-                high, lowp = split(b[kind])
-                yt[16 * g : 16 * g + 16, spot(kind)] = high
-                yt[128 + 16 * g : 144 + 16 * g, spot(kind)] = lowp
+        for g, block in enumerate(blocks):
+            for b, moved in enumerate((block, times(block, run))):
+                for kind in range(2):
+                    high, lowp = split(moved[kind])
+                    yt[b, 16 * g : 16 * g + 16, spot(kind)] = high
+                    yt[b, 128 + 16 * g : 144 + 16 * g, spot(kind)] = lowp
 
         sin_b, cos_b = sincos(along_x * (rowf + 0.5))
         more = times((cos_b, sin_b), (cos_m[7:8], sin_m[7:8]))
@@ -349,7 +372,7 @@
         sx = jnp.concatenate([sin_b, more[1]], 0)
         nx = -sx
         before_x = (cos_m[5:6], -sin_m[5:6])
-        for t in range(n_x):
+        for t in range(n_a):
             pq = w * cos_m[t : t + 1] + turned * sin_m[t : t + 1]
 
             def put_left(r, k, value):
@@ -366,9 +389,10 @@
                         put_left((kind * 4 + c) * half, k, products[kind][k])
                 if c == 2:
                     for kind in range(2):
-                        cols[t, kind] = cols[t, kind] + (
-                            products[kind][0] * before_y[0] + products[kind][1] * before_y[1]
-                        )
+                        for b, edge in enumerate(before_y):
+                            cols[2 * t + b, kind] = cols[2 * t + b, kind] + (
+                                products[kind][0] * edge[0] + products[kind][1] * edge[1]
+                            )
                 if c == 3:
                     ox, oy = before_x
                     put_left(128, 0, jnp.broadcast_to(p * ox + nq * oy, (16, 128)))
@@ -379,37 +403,37 @@
         share(other).start()
         return carry
 
-    def answer_late():
-        def one(i, carry):
-            return answer(jnp.where(is_far, n_z - 1 - i, n_half + i), carry)
-
-        lax.fori_loop(0, n_half, one, 0)
-
-    def own_planes(i, carry):
-        other = own_half + ((z + 1 + i) & (n_half - 1))
-
-        @pl.when(jnp.logical_or(other < z, jnp.logical_and(other > z, jnp.logical_not(is_far))))
+    def first_planes(i, carry):
+        other = jnp.where(is_far, n_z - 1 - i, first_half + ((z + 1 + i) & (n_half - 1)))
+
+        @pl.when(other != z)
         def _():
             arrival(other).wait_recv()
 
-        @pl.when(jnp.logical_and(other > z, jnp.logical_not(is_far)))
+        @pl.when(other > z)
         def _():
             share(other).start()
 
-        operands(other, other - own_half)
-        return carry
-
-    def other_planes(i, carry):
-        @pl.when(is_late)
+        operands(other, other - first_half)
+        return carry
+
+    def second_planes(i, carry):
+        other = second_half + i
+
+        @pl.when(jnp.logical_or(other < z, is_near))
         def _():
-            arrival(i).wait_recv()
-
-        operands(other_half + i, i)
+            arrival(other).wait_recv()
+
+        @pl.when(is_near)
+        def _():
+            share(other).start()
+
+        operands(other, i)
         return carry
 
     def tile(t):
         both = lax.dot_general(
-            lt[t], yt[...], (((1,), (1,)), ((), ())), preferred_element_type=F32
+            lt[t // 2], yt[t & 1], (((1,), (1,)), ((), ())), preferred_element_type=F32
         )
         main = both[0:136, 0:128] + (both[0:136, 128:256] + both[144:280, 0:128])
         before = jnp.zeros((1, 128), F32)
@@ -421,16 +445,16 @@
         return main[0:128], jnp.where(row8 == 0, main[128:136], jnp.where(row8 == 1, before, 0.0))
 
     cols[...] = jnp.zeros(cols.shape, F32)
-    own_half = (z // n_half) * n_half
-    other_half = n_half - own_half
+    is_near = z < n_half // 2
     is_far = jnp.logical_and(z >= n_half // 2, jnp.logical_not(is_late))
+    first_half = jnp.where(is_near, 0, n_half)
+    second_half = n_half - first_half
 
     @pl.when(is_far)
     def _():
         lax.fori_loop(z + 1, n_half, answer, 0)
-        answer_late()
-
-    lax.fori_loop(0, n_half, own_planes, 0)
+
+    lax.fori_loop(0, n_half, first_planes, 0)
 
     def first_pass(k, carry):
         main, rest = tile((x + k) & (n_x - 1))
@@ -440,18 +464,20 @@
 
     lax.fori_loop(0, n_x, first_pass, 0)
 
-    when(jnp.logical_not(is_late), magnetic)
-    when(z < n_half // 2, answer_late)
-    lax.fori_loop(0, n_half, other_planes, 0)
+    lax.fori_loop(0, n_half, second_planes, 0)
 
     def to_x(k):
         return copy_to(
-            acc.at[k], from_x.at[k - 1], x_send.at[k - 1], x_recv.at[k - 1], column_of(k)
+            acc.at[k], from_x.at[spot_x + k], x_send.at[k], x_recv.at[spot_x + k],
+            {"gy": ((x + k) & (n_x - 1)) * n_hi + z_hi, "gz": 2 * y + 1},
         )
 
-    @pl.when(x < n_x - 1)
-    def _():
-        pl.semaphore_wait(x_token, n_x - 1 - x)
+    spot_x = jnp.where(adds, 0, n_x)
+    tokens = n_x - x - core
+
+    @pl.when(tokens > 0)
+    def _():
+        pl.semaphore_wait(x_token, tokens)
 
     def second_pass(i, carry):
         k = jnp.where(i == n_x - 1, 0, jnp.where(i == 0, n_x // 2, jnp.where(i == 1, 1, i + 1)))
@@ -459,13 +485,14 @@
         acc[k, 0:128] = acc[k, 0:128] + main
         acc[k, 128:136] = acc[k, 128:136] + rest
 
-        @pl.when(k > 0)
+        @pl.when(jnp.logical_or(k > 0, jnp.logical_not(adds)))
         def _():
             to_x(k).start()
 
         return carry
 
     lax.fori_loop(0, n_x, second_pass, 0)
+    when(jnp.logical_not(is_late), magnetic)
 
     @pl.when(wrap_high)
     def _():
@@ -485,19 +512,25 @@
             )
         send_hx_hz()
 
-    for k in range(1, n_x):
-        to_x(k).wait_recv()
-    total[...] = sum((from_x[k] for k in range(n_x - 1)), acc[0])
-
     def to_top(k):
         return copy_to(
             total, from_gz.at[k], gz_send.at[0], gz_recv.at[k], {"gz": n_gz - 1}
         )
 
-    @pl.when(jnp.logical_not(is_top))
+    @pl.when(adds)
+    def _():
+        for k in range(1, 2 * n_x):
+            copy_to(
+                acc.at[0], from_x.at[k], x_send.at[0], x_recv.at[k], {"gz": 2 * y}
+            ).wait_recv()
+        total[...] = sum((from_x[k] for k in range(1, 2 * n_x)), acc[0])
+
+    sends_up = jnp.logical_and(adds, jnp.logical_not(is_top))
+
+    @pl.when(sends_up)
     def _():
         pl.semaphore_wait(top_token, 1)
-        to_top(gz).start()
+        to_top(y).start()
 
     for load in loads[6:]:
         load.wait()
@@ -508,6 +541,7 @@
     y_packed = jnp.where(low_y, ky_in[...], 0.0)
     z_edges = [jnp.where(low_z, kz_in[i], 0.0) for i in range(2)]
     missing = jnp.where(wrap_high, COURANT, 0.0)
+    when(low_z, ez_copy.wait_send)
 
     def chosen(which, m):
         value = jnp.full(m.shape, table[which, 3], F32)
@@ -538,17 +572,32 @@
         for i, e in enumerate((ex, ey, ez)):
             pole = p_buf[i, j]
             after = decay * pole + drive * e
-            p_out[i, j] = after
-            e_out[i, j] = e + coef * (side[i] - 0.5 * (after + pole))
-            h_out[i, j] = h_buf[i, j]
+            p_buf[i, j] = after
+            e_buf[i, j] = e + coef * (side[i] - 0.5 * (after + pole))
+
+    last = depth - 1
+    stores = [
+        pltpu.make_async_copy(a, b, store_sem.at[k])
+        for k, (a, b) in enumerate(
+            (
+                (p_buf, p_out),
+                (h_buf.at[:, 0:last], h_out.at[:, 0:last]),
+                (e_buf.at[:, 0:last], e_out.at[:, 0:last]),
+                (h_buf.at[:, last], h_out.at[:, last]),
+                (e_buf.at[:, last], e_out.at[:, last]),
+            )
+        )
+    ]
+    for store in stores[:3]:
+        store.start()
 
     @pl.when(is_top)
     def _():
-        for k in range(n_gz - 1):
+        for k in range(n_y - 1):
             copy_to(
                 total, from_gz.at[k], gz_send.at[0], gz_recv.at[k], {"gz": 0}
             ).wait_recv()
-        summed = sum((from_gz[k] for k in range(n_gz - 1)), total[...])
+        summed = sum((from_gz[k] for k in range(n_y - 1)), total[...])
 
         def unfold(even, odd, spot):
             lower = even - odd
@@ -574,15 +623,19 @@
             for kind in range(2)
         ]
         near_y = unfold(sides[0], sides[1], 4)
-        last = depth - 1
         coef = chosen(2, m_buf[last])
-        h_out[0, last] = h_out[0, last] - COURANT * src[2]
-        h_out[1, last] = h_out[1, last] - COURANT * src[3]
+        h_buf[0, last] = h_buf[0, last] - COURANT * src[2]
+        h_buf[1, last] = h_buf[1, last] - COURANT * src[3]
         behind_x = src[3] - jnp.where(row == 0, near_x, pltpu.roll(src[3], 1, 0))
         behind_y = src[2] - jnp.where(lane == 0, near_y, pltpu.roll(src[2], 1, 1))
-        e_out[0, last] = e_out[0, last] + coef * (COURANT * src[3] - src[0])
-        e_out[1, last] = e_out[1, last] - coef * (COURANT * src[2] + src[1])
-        e_out[2, last] = e_out[2, last] - coef * (COURANT * (behind_x - behind_y))
+        e_buf[0, last] = e_buf[0, last] + coef * (COURANT * src[3] - src[0])
+        e_buf[1, last] = e_buf[1, last] - coef * (COURANT * src[2] + src[1])
+        e_buf[2, last] = e_buf[2, last] - coef * (COURANT * (behind_x - behind_y))
+
+    for store in stores[3:]:
+        store.start()
+    for store in stores:
+        store.wait()
 
     def sent(other, carry):
         @pl.when(other != z)
@@ -594,13 +647,13 @@
     lax.fori_loop(0, n_z, sent, 0)
     for k in range(1, n_x):
         to_x(k).wait_send()
+    when(jnp.logical_not(adds), to_x(0).wait_send)
     when(low_x, ex_copy.wait_send)
     when(low_y, ey_copy.wait_send)
-    when(low_z, ez_copy.wait_send)
     when(high_x, hx_copy.wait_send)
     when(high_y, hy_copy.wait_send)
     when(high_z, hz_copy.wait_send)
-    when(jnp.logical_not(is_top), to_top(gz).wait_send)
+    when(sends_up, to_top(y).wait_send)
 
 
 def put(*refs):
@@ -626,7 +679,7 @@
         functools.partial(kernel, sizes),
         out_shape=(field, field, field),
         in_specs=[hbm] * 9,
-        out_specs=(vmem, vmem, vmem),
+        out_specs=(hbm, hbm, hbm),
         scratch_shapes=[
             pltpu.VMEM((8, 8, 16), F32),
             pltpu.SMEM((2, 8), F32),
@@ -638,13 +691,13 @@
             pltpu.VMEM(block, F32),
             pltpu.VMEM((depth, width_x, width_y), jnp.int32),
             pltpu.VMEM((n_z, 16, 128), F32),
-            pltpu.VMEM((256, n_z * 128), BF16),
-            pltpu.VMEM((n_x, 288, n_z * 128), BF16),
+            pltpu.VMEM((2, 256, n_z * 128), BF16),
+            pltpu.VMEM((n_x // 2, 288, n_z * 128), BF16),
             pltpu.VMEM((n_x, 2, half, 128), F32),
             pltpu.VMEM((n_x, 136, 128), F32),
-            pltpu.VMEM((n_x - 1, 136, 128), F32),
+            pltpu.VMEM((2 * n_x, 136, 128), F32),
             pltpu.VMEM((136, 128), F32),
-            pltpu.VMEM((n_gz - 1, 136, 128), F32),
+            pltpu.VMEM((max(n_gz // 2 - 1, 1), 136, 128), F32),
             pltpu.VMEM((5, half, 128), F32),
             pltpu.VMEM((8, 128), F32),
             pltpu.VMEM((8, 128), F32),
@@ -657,12 +710,13 @@
             pltpu.VMEM((8, 128), F32),
             pltpu.VMEM((2, width_x, 128), F32),
             dma((9,)),
+            dma((5,)),
             dma((n_z,)),
             dma((n_z,)),
-            dma((n_x - 1,)),
-            dma((n_x - 1,)),
+            dma((n_x,)),
+            dma((2 * n_x,)),
             dma((1,)),
-            dma((n_gz - 1,)),
+            dma((max(n_gz // 2 - 1, 1),)),
             dma((6,)),
             dma((6,)),
             pltpu.SemaphoreType.REGULAR,

time: 37.5 us -> 35.4 us (0.944)
  the two profiles are of different devices: /device:TPU:153 before, /device:TPU:281 now
where the time goes in v5:
time: 35.4 us; the launch traced here: 35.3 us
  Pallas kernels  34.6 us (98%)
  between operations  0.64 us (2%)
    pallas_call x1, Pallas kernels, local(): pl.pallas_call(functools.partial(kernel, sizes), out_shape=(field, field,...  32.7 us
    pallas_call x1, Pallas kernels, local(): pl.pallas_call(put, out_shape=(field, field, field), in_specs=[vmem] * 3,...  1.94 us

profile of v5, /device:TPU:281, one launch (start us, length us, event | category | flops | bytes accessed | tf_op | source)
XLA Modules:
  0.0 35.3 jit_solution(4650196992760761457)
XLA Ops:
  0.6 32.7 %shard_map.112 = (f32[3,4,32,128]{3,2,1,0:T(8,128)}, f32[3,4,32,128]{3,2,1,0:T(8,128)}, f32[3,4,32,128]{3,2,1,0:T(8,128)}) custom-call(f32[8,8,16]{2,1,0:T(8,128)} %bitcast.1, f32[2,8]{1,0:T(2,128)} %cosines_in.1, f32[16]{0:T(128)} %wave_in.1, f32[16]{0:T(128)} %phase_in.1, f32[3,4]{1,0:T(4,128)} %table_in.1, f32[3,4,32,128]{3,2,1,0:T(8,128)} %e_in.1, ...), custom_call_target="tpu_custom_call" | custom-call | tf_op jit(solution)/shard_map/pallas_call | solution.py:678
  33.3 1.9 %shard_map.113 = (f32[3,4,32,128]{3,2,1,0:T(8,128)}, f32[3,4,32,128]{3,2,1,0:T(8,128)}, f32[3,4,32,128]{3,2,1,0:T(8,128)}) custom-call(f32[3,4,32,128]{3,2,1,0:T(8,128)} %get-tuple-element.6.refs_0_, f32[3,4,32,128]{3,2,1,0:T(8,128)} %get-tuple-element.7.refs_1_, f32[3,4,32,128]{3,2,1,0:T(8,128)} %get-tuple-element.8.refs_2_), custom_call_target="tpu_custom_call" | custom-call | tf_op jit(solution)/shard_map/pallas_call | solution.py:730

commit v6 on v5

--- a/solution.py
+++ b/solution.py
@@ -102,7 +102,7 @@
             )
         )
     ]
-    for load in loads:
+    for load in loads[:4]:
         load.start()
 
     wrap_low = jnp.logical_and(z_hi == n_hi - 1, x < n_x - 1)
@@ -113,11 +113,11 @@
     def greet(device):
         pl.semaphore_signal(barrier, inc=1, device_id=device, device_id_type=MESH)
 
-    def greet_plane(other, carry):
-        greet(plane(other))
-        return carry
-
-    lax.fori_loop(z + 1, n_z, greet_plane, 0)
+    def greet_plane(i, carry):
+        greet(plane(n_z - 1 - i))
+        return carry
+
+    lax.fori_loop(0, n_z - 1 - z, greet_plane, 0)
 
     def greet_column(other, carry):
         greet({"gy": other * n_hi + z_hi, "gz": 2 * y + 1})
@@ -159,6 +159,8 @@
         + wrap_low.astype(jnp.int32)
     )
 
+    for load in loads[4:]:
+        load.start()
     for load in loads[:4]:
         load.wait()
     row8 = iota((8, 128), 0)
@@ -591,6 +593,23 @@
     for store in stores[:3]:
         store.start()
 
+    def sent(other, carry):
+        @pl.when(other != z)
+        def _():
+            share(other).wait_send()
+
+        return carry
+
+    lax.fori_loop(0, n_z, sent, 0)
+    for k in range(1, n_x):
+        to_x(k).wait_send()
+    when(jnp.logical_not(adds), to_x(0).wait_send)
+    when(low_x, ex_copy.wait_send)
+    when(low_y, ey_copy.wait_send)
+    when(high_x, hx_copy.wait_send)
+    when(high_y, hy_copy.wait_send)
+    when(high_z, hz_copy.wait_send)
+
     @pl.when(is_top)
     def _():
         for k in range(n_y - 1):
@@ -637,22 +656,6 @@
     for store in stores:
         store.wait()
 
-    def sent(other, carry):
-        @pl.when(other != z)
-        def _():
-            share(other).wait_send()
-
-        return carry
-
-    lax.fori_loop(0, n_z, sent, 0)
-    for k in range(1, n_x):
-        to_x(k).wait_send()
-    when(jnp.logical_not(adds), to_x(0).wait_send)
-    when(low_x, ex_copy.wait_send)
-    when(low_y, ey_copy.wait_send)
-    when(high_x, hx_copy.wait_send)
-    when(high_y, hy_copy.wait_send)
-    when(high_z, hz_copy.wait_send)
     when(sends_up, to_top(y).wait_send)
 
 

time: 35.4 us -> 35.3 us (level)
  no operation moved by 1% of the time
where the time goes in v6:
time: 35.3 us; the launch traced here: 35.1 us
  Pallas kernels  34.4 us (97%)
  between operations  0.64 us (2%)
    pallas_call x1, Pallas kernels, local(): pl.pallas_call(functools.partial(kernel, sizes), out_shape=(field, field,...  32.5 us
    pallas_call x1, Pallas kernels, local(): pl.pallas_call(put, out_shape=(field, field, field), in_specs=[vmem] * 3,...  1.94 us

profile of v6, /device:TPU:281, one launch (start us, length us, event | category | flops | bytes accessed | tf_op | source)
XLA Modules:
  0.0 35.1 jit_solution(1631241152324521687)
XLA Ops:
  0.6 32.5 %shard_map.112 = (f32[3,4,32,128]{3,2,1,0:T(8,128)}, f32[3,4,32,128]{3,2,1,0:T(8,128)}, f32[3,4,32,128]{3,2,1,0:T(8,128)}) custom-call(f32[8,8,16]{2,1,0:T(8,128)} %bitcast.1, f32[2,8]{1,0:T(2,128)} %cosines_in.1, f32[16]{0:T(128)} %wave_in.1, f32[16]{0:T(128)} %phase_in.1, f32[3,4]{1,0:T(4,128)} %table_in.1, f32[3,4,32,128]{3,2,1,0:T(8,128)} %e_in.1, ...), custom_call_target="tpu_custom_call" | custom-call | tf_op jit(solution)/shard_map/pallas_call | solution.py:681
  33.1 1.9 %shard_map.113 = (f32[3,4,32,128]{3,2,1,0:T(8,128)}, f32[3,4,32,128]{3,2,1,0:T(8,128)}, f32[3,4,32,128]{3,2,1,0:T(8,128)}) custom-call(f32[3,4,32,128]{3,2,1,0:T(8,128)} %get-tuple-element.6.refs_0_, f32[3,4,32,128]{3,2,1,0:T(8,128)} %get-tuple-element.7.refs_1_, f32[3,4,32,128]{3,2,1,0:T(8,128)} %get-tuple-element.8.refs_2_), custom_call_target="tpu_custom_call" | custom-call | tf_op jit(solution)/shard_map/pallas_call | solution.py:733
